TPU v7x, 32 devices: a whole 2x2x4 slice. The times are simulated.
32 devices in a mesh: tm: 2 (over x), heads: 4 (over y, core), rep: 4 (over z).
Axes of the slice: x: 2, y: 2, z: 4, core: 2. Of those that a mesh axis runs over, the one named last changes fastest.
Arguments:
- queries: bfloat16 [2048, 2560], P(('tm', 'rep'), 'heads'), may hold values from -100 to 100
- keys: bfloat16 [2048, 2560], P(('tm', 'rep'), 'heads'), may hold values from -4 to 4
- values: bfloat16 [2048, 2560], P(('tm', 'rep'), 'heads'), may hold values from -6 to 6
- block_lists: int32 [16, 16], P(('tm', 'rep')), may hold values from 0 to 15, as said below
- list_counts: int32 [16], P(('tm', 'rep')), may hold values from 2 to 16, as said below
- out_weight: bfloat16 [2560, 5120], P('heads', 'rep'), may hold values from -0.125 to 0.125
- gate: float32 [5120], P('rep'), may hold values from 0.5 to 2
Outputs:
- branch: bfloat16 [2048, 5120], P(('tm', 'heads'), 'rep')
Inputs may be any that keep to these rules, and one draw needn't show every extreme that they name: `block_lists`: entry 0 of block b's list is b itself; only the first list_counts[b] entries count, the rest are arbitrary block numbers. `list_counts`: every draw has a block whose count is 16.
All inputs are finite; a program needn't handle non-finite values.
Results may differ from a plain program's by a relative error of at most 0.0085.
Values may be sent and summed in bfloat16 or wider, within the bound.
A program may use at most 64 MiB of HBM per device.

v0:
```python
import jax
import jax.numpy as jnp
from jax import lax
from jax.sharding import PartitionSpec as P

HD = 128
BLOCK = 128
LIST = 16


def from_behind(value, axis, steps):
    count = lax.axis_size(axis)
    pairs = [(source, (source + steps) % count) for source in range(count)]
    return lax.ppermute(value, axis, pairs)


def shards(queries, keys, values, block_lists, list_counts, out_weight, gate):
    tok_rows = queries.shape[0]
    head_count = queries.shape[1] // HD
    group_size = lax.axis_size("rep")
    cycle_size = lax.axis_size("tm")
    rep_index = lax.axis_index("rep")
    tm_index = lax.axis_index("tm")
    all_queries, all_lists, all_counts = (
        lax.all_gather(queries, "rep", axis=0, tiled=True),
        lax.all_gather(block_lists, "rep", axis=0, tiled=True),
        lax.all_gather(list_counts, "rep", axis=0, tiled=True),
    )
    query_span = all_queries.shape[0]
    query_blocks = all_lists.shape[0]
    total_blocks = query_blocks * cycle_size
    local_blocks = tok_rows // BLOCK
    slot_used = jnp.arange(LIST)[None, :] < all_counts[:, None]
    block_ids = jnp.arange(total_blocks, dtype=jnp.int32)
    block_mask = jnp.any(
        (all_lists[:, :, None] == block_ids[None, None, :]) & slot_used[:, :, None], axis=1
    )
    query_heads = all_queries.reshape(query_span, head_count, HD)
    logit_scale = 1.0 / HD**0.5

    def absorb(softmax_state, key_value, source_frame):
        running_max, running_sum, running_acc = softmax_state
        key_part = key_value[0].reshape(tok_rows, head_count, HD)
        value_part = key_value[1].reshape(tok_rows, head_count, HD)
        first_block = (source_frame * group_size + rep_index) * local_blocks
        block_cols = lax.dynamic_slice_in_dim(block_mask, first_block, local_blocks, 1)
        attention_logits = (
            jnp.einsum("qhd,khd->hqk", query_heads, key_part, preferred_element_type=jnp.float32)
            * logit_scale
        )
        shaped = attention_logits.reshape(head_count, query_blocks, BLOCK, local_blocks, BLOCK)
        permitted = jnp.broadcast_to(block_cols[None, :, None, :, None], shaped.shape).reshape(
            head_count, query_span, tok_rows
        )
        masked = jnp.where(permitted, attention_logits, -1e30)
        new_max = jnp.maximum(running_max, jnp.max(masked, axis=2).T)
        weights = jnp.where(permitted, jnp.exp(masked - new_max.T[:, :, None]), 0.0)
        rescale = jnp.exp(running_max - new_max)
        running_sum = running_sum * rescale + jnp.sum(weights, axis=2).T
        contribution = jnp.einsum(
            "hqk,khd->qhd",
            weights.astype(jnp.bfloat16),
            value_part,
            preferred_element_type=jnp.float32,
        )
        running_acc = running_acc * rescale[:, :, None] + contribution
        return (new_max, running_sum, running_acc)

    softmax_state = (
        jnp.full((query_span, head_count), -1e30, jnp.float32),
        jnp.zeros((query_span, head_count), jnp.float32),
        jnp.zeros((query_span, head_count, HD), jnp.float32),
    )
    key_value = jnp.stack([keys, values])
    softmax_state = absorb(softmax_state, key_value, tm_index)

    def both_turn(turn_index, carry):
        current_state, ahead_pair, behind_pair = carry
        ahead_pair = from_behind(ahead_pair, "tm", 1)
        behind_pair = from_behind(behind_pair, "tm", -1)
        current_state = absorb(current_state, ahead_pair, (tm_index - turn_index - 1) % cycle_size)
        current_state = absorb(current_state, behind_pair, (tm_index + turn_index + 1) % cycle_size)
        return (current_state, ahead_pair, behind_pair)

    softmax_state, ahead_pair, behind_pair = lax.fori_loop(
        0, cycle_size // 2 - 1, both_turn, (softmax_state, key_value, key_value)
    )
    ahead_pair = from_behind(ahead_pair, "tm", 1)
    softmax_state = absorb(softmax_state, ahead_pair, (tm_index + cycle_size // 2) % cycle_size)
    running_max, running_sum, running_acc = softmax_state
    part_max, part_sum, part_acc = (
        lax.all_to_all(running_max[None], "rep", split_axis=1, concat_axis=0, tiled=True),
        lax.all_to_all(running_sum[None], "rep", split_axis=1, concat_axis=0, tiled=True),
        lax.all_to_all(running_acc[None], "rep", split_axis=1, concat_axis=0, tiled=True),
    )
    overall_max = jnp.max(part_max, axis=0)
    factor = jnp.exp(part_max - overall_max[None])
    denominator = jnp.sum(factor * part_sum, axis=0)
    weighted_value_sum = jnp.sum(factor[:, :, :, None] * part_acc, axis=0)
    attended = (
        (weighted_value_sum / denominator[:, :, None])
        .reshape(tok_rows, head_count * HD)
        .astype(jnp.bfloat16)
    )
    partial_out = jnp.dot(
        lax.all_gather(attended, "rep", axis=0, tiled=True),
        out_weight,
        preferred_element_type=jnp.float32,
    )
    summed = lax.psum_scatter(partial_out, "heads", scatter_dimension=0, tiled=True)
    return (gate[None, :] * summed).astype(jnp.bfloat16)


def solution(mesh):
    placed = (
        P(("tm", "rep"), "heads"),
        P(("tm", "rep"), "heads"),
        P(("tm", "rep"), "heads"),
        P(("tm", "rep"), None),
        P(("tm", "rep")),
        P("heads", "rep"),
        P("rep"),
    )
    return jax.shard_map(
        shards, mesh=mesh, in_specs=placed, out_specs=P(("tm", "heads"), "rep"), check_vma=False
    )
```

profile of v0, /device:TPU:0, one launch (start us, length us, event | category | flops | bytes accessed | tf_op | source)
XLA Modules:
  0.0 250.4 jit_solution(15367953572377515439)
XLA Ops:
  6.5 2.0 copy.91
  8.6 1.1 copy.97
  9.7 1.3 copy.92
  11.0 0.9 pad_maximum_fusion
  11.9 2.9 %collective-permute-start = (bf16[2,256,640]{1,2,0:T(8,128)(2,1)}, bf16[2,256,640]{1,2,0:T(8,128)(2,1)S(1)}, u32[]{:S(2)}, u32[]{:S(2)}) collective-permute-start(bf16[2,256,640]{1,2,0:T(8,128)(2,1)} %pad_maximum_fusion), channel_id=1, source_target_pairs={{0,16},{16,0},{1,17},{17,1},{2,18},{18,2},{3,19},{19,3},{4,20},{20... | collective-permute-start | bytes 1966088 | tf_op jit(solution)/shard_map/ppermute | solution.py:14
  14.8 1.2 dynamic-slice
  16.6 0.9 dynamic-update-slice
  17.5 10.0 %all-reduce = s32[8]{0:T(128)S(1)} all-reduce(s32[8]{0:T(128)S(1)} %dynamic-update-slice), channel_id=1, replica_groups=mesh['tm'=2,'heads'=4,'rep'=4] {'rep'}, use_global_device_ids=true, to_apply=%add | all-reduce | flops 8 | bytes 64
  27.4 8.3 %all-gather = s32[4,2,16]{2,1,0:T(2,128)S(1)} all-gather(s32[1,2,16]{2,1,0:T(2,128)} %bitcast.129), channel_id=1, replica_groups=mesh['tm'=2,'heads'=4,'rep'=4] {'rep'}, dimensions={0}, use_global_device_ids=true | all-gather | bytes 640 | tf_op jit(solution)/shard_map/all_gather | solution.py:26
  36.8 0.8 fusion.39
  37.6 7.6 %all-gather.4.cloned.1.call-done = bf16[1024,640]{0,1:T(8,128)(2,1)} async-done(((bf16[256,640]{0,1:T(8,128)(2,1)}), bf16[1024,640]{0,1:T(8,128)(2,1)}) %all-gather.4.cloned.1.call-update) | async-done | bytes 1310736 | tf_op jit(solution)/shard_map/all_gather | solution.py:25
  45.2 2.6 %fusion = (f32[5,1024]{1,0:T(8,128)S(1)}, f32[5,1024,256]{1,2,0:T(8,128)S(1)}) fusion(pred[1024,256]{0,1:T(8,128)(4,1)S(1)} %bitcast.115, bf16[1024,5,128]{0,2,1:T(8,128)(2,1)} %bitcast.106, bf16[256,5,128]{0,2,1:T(8,128)(2,1)S(1)} %bitcast.111), kind=kOutput, calls=%fused_computation.4 | convolution fusion | flops 339471360 | bytes 7163904 | tf_op jit(solution)/shard_map/qhd,khd->hqk/dot_general | solution.py:48
  47.9 1.2 fusion.1
  49.2 2.6 %fusion.2 = (f32[5,1024]{1,0:T(8,128)S(1)}, f32[5,1024]{1,0:T(8,128)S(1)}) fusion(f32[5,1024,256]{1,2,0:T(8,128)S(1)} %get-tuple-element.20, f32[5,1024]{1,0:T(8,128)S(1)} %get-tuple-element.14, pred[1024,256]{0,1:T(8,128)(4,1)S(1)} %bitcast.116, f32[5,1024]{1,0:T(8,128)S(1)} %get-tuple-element.13, f32[5,256,1024]{2,1,0:T(8,128)S(1)} %get-tuple-element.18, ...), kind=kLoop, calls=%fused_computation.6 | loop fusion | flops 13096960 | bytes 11091968 | tf_op jit(solution)/shard_map/reduce_sum | solution.py:59
  53.4 1.9 reduce
  55.3 1.0 reshape.74
  56.3 3.3 %all-to-all-start.2 = ((f32[4,1,1280]{2,1,0:T(1,128)}), f32[4,1,1280]{2,1,0:T(1,128)S(1)}, u32[]{:S(2)}, u32[]{:S(2)}) async-start(f32[4,1,1280]{2,1,0:T(1,128)} %reshape.74), calls=%async_computation.2 | async-start | bytes 40960 | tf_op jit(solution)/shard_map/all_to_all | solution.py:93
  59.6 5.8 %fusion.8 = f32[5,1024,128]{2,1,0:T(8,128)} fusion(bf16[256,5,128]{0,2,1:T(8,128)(2,1)S(1)} %bitcast.123, f32[5,1024,256]{1,2,0:T(8,128)} %copy-done.2, f32[5,1024]{1,0:T(8,128)} %copy-done.8, pred[1024,256]{0,1:T(8,128)(4,1)S(1)} %bitcast.117), kind=kOutput, calls=%fused_computation.11 | convolution fusion | flops 342097920 | bytes 8474624 | tf_op jit(solution)/shard_map/hqk,khd->qhd/dot_general | solution.py:60
  65.7 1.9 reduce.2
  67.7 1.0 reshape.72
  68.6 5.0 %all-to-all-start = ((f32[4,1,1280]{2,1,0:T(1,128)}), f32[4,1,1280]{2,1,0:T(1,128)S(1)}, u32[]{:S(2)}, u32[]{:S(2)}) async-start(f32[4,1,1280]{2,1,0:T(1,128)} %reshape.72), calls=%async_computation | async-start | bytes 40960 | tf_op jit(solution)/shard_map/all_to_all | solution.py:92
  73.7 5.3 %fusion.10 = f32[1,1024,5,128]{3,1,2,0:T(8,128)S(1)} fusion(f32[5,1024,128]{2,1,0:T(8,128)} %fusion.8, bf16[256,5,128]{0,2,1:T(8,128)(2,1)} %bitcast.127, f32[5,256,1024]{2,1,0:T(8,128)} %copy-done.1, f32[5,1024]{1,0:T(8,128)S(1)} %copy-done.7, pred[1024,256]{0,1:T(8,128)(4,1)S(1)} %bitcast.114, f32[1024,5]{0,1:T(8,128)S(1)} %copy-done.10, ...), kind=kOutput, calls=%fused_computation.13 | convolution fusion | flops 344064000 | bytes 11137024 | tf_op jit(solution)/shard_map/hqk,khd->qhd/dot_general | solution.py:60
  79.0 4.2 %copy.107 = f32[1,1024,5,128]{3,0,2,1:T(1,128)} copy(f32[1,1024,5,128]{3,1,2,0:T(8,128)S(1)} %fusion.10) | data formatting | bytes 5242880 | tf_op jit(solution)/shard_map/broadcast_in_dim | solution.py:94
  83.2 5.1 %all-to-all-start.1 = ((f32[1,1024,5,128]{3,0,2,1:T(1,128)}), f32[1,1024,5,128]{3,0,2,1:T(1,128)}, u32[]{:S(2)}, u32[]{:S(2)}) async-start(f32[1,1024,5,128]{3,0,2,1:T(1,128)} %copy.107), calls=%async_computation.1 | async-start | bytes 5242880 | tf_op jit(solution)/shard_map/all_to_all | solution.py:94
  91.7 54.2 %all-to-all-done.1 = f32[1,1024,5,128]{3,0,2,1:T(1,128)} async-done(((f32[1,1024,5,128]{3,0,2,1:T(1,128)}), f32[1,1024,5,128]{3,0,2,1:T(1,128)}, u32[]{:S(2)}, u32[]{:S(2)}) %all-to-all-start.1) | async-done | bytes 2621472 | tf_op jit(solution)/shard_map/all_to_all | solution.py:94
  145.9 1.9 copy.108
  147.8 0.9 multiply_reduce_fusion
  149.0 0.9 copy.111
  150.0 35.7 %all-gather.6.cloned.1.call-done = bf16[1024,640]{0,1:T(8,128)(2,1)} async-done(((bf16[256,640]{0,1:T(8,128)(2,1)}), bf16[1024,640]{0,1:T(8,128)(2,1)}) %all-gather.6.cloned.1.call-update) | async-done | bytes 1310736 | tf_op jit(solution)/shard_map/all_gather | solution.py:106
  185.7 5.9 %fusion.40 = f32[1024,1280]{1,0:T(8,128)} fusion(bf16[1024,640]{0,1:T(8,128)(2,1)} %all-gather.6.cloned.1.call-done, bf16[640,1280]{1,0:T(8,128)(2,1)S(1)} %copy-done), kind=kOutput, calls=%fused_computation.60 | convolution fusion | flops 1677721600 | bytes 8192000 | tf_op jit(solution)/shard_map/dot_general | solution.py:105
  191.6 50.1 %reduce-scatter.2.cloned.1.call-done = f32[256,1280]{1,0:T(8,128)} async-done(((f32[1024,1280]{1,0:T(8,128)}), f32[256,1280]{1,0:T(8,128)}) %reduce-scatter.2.cloned.1.call-update) | async-done | bytes 1310736 | tf_op jit(solution)/shard_map/reduce_scatter | solution.py:110
  241.7 2.2 multiply_convert_fusion
  (60 shorter events, 6.6 us)
Async XLA Ops:
  6.5 179.2 %copy-start = (bf16[640,1280]{1,0:T(8,128)(2,1)S(1)}, bf16[640,1280]{1,0:T(8,128)(2,1)}, u32[]{:S(2)}) copy-start(bf16[640,1280]{1,0:T(8,128)(2,1)} %param.12) | copy-start | bytes 4915204
  6.5 38.7 %all-gather.4.cloned.1.call-start = ((), (), s32[]{:S(2)}) async-start(), calls=%async_computation.4 | async-start | bytes 1638400 | tf_op jit(solution)/shard_map/all_gather | solution.py:25
  9.7 26.6 %copy-start.4 = (bf16[256,640]{0,1:T(8,128)(2,1)}, bf16[256,640]{0,1:T(8,128)(2,1)S(1)}, u32[]{:S(2)}) copy-start(bf16[256,640]{0,1:T(8,128)(2,1)S(1)} %copy.97) | copy-start | bytes 983044
  11.9 24.9 %collective-permute-start = (bf16[2,256,640]{1,2,0:T(8,128)(2,1)}, bf16[2,256,640]{1,2,0:T(8,128)(2,1)S(1)}, u32[]{:S(2)}, u32[]{:S(2)}) collective-permute-start(bf16[2,256,640]{1,2,0:T(8,128)(2,1)} %pad_maximum_fusion), channel_id=1, source_target_pairs={{0,16},{16,0},{1,17},{17,1},{2,18},{18,2},{3,19},{19,3},{4,20},{20... | collective-permute-start | bytes 1966088 | tf_op jit(solution)/shard_map/ppermute | solution.py:14
  45.2 2.6 %copy-start.3 = (bf16[1024,640]{0,1:T(8,128)(2,1)S(1)}, bf16[1024,640]{0,1:T(8,128)(2,1)}, u32[]{:S(2)}) copy-start(bf16[1024,640]{0,1:T(8,128)(2,1)} %all-gather.4.cloned.1.call-done) | copy-start | bytes 3932164
  47.9 4.0 %copy-start.2 = (f32[5,1024,256]{1,2,0:T(8,128)}, f32[5,1024,256]{1,2,0:T(8,128)S(1)}, u32[]{:S(2)}) copy-start(f32[5,1024,256]{1,2,0:T(8,128)S(1)} %get-tuple-element.20) | copy-start | bytes 15728644
  49.1 2.7 %copy-start.1 = (f32[5,256,1024]{2,1,0:T(8,128)}, f32[5,256,1024]{2,1,0:T(8,128)S(1)}, u32[]{:S(2)}) copy-start(f32[5,256,1024]{2,1,0:T(8,128)S(1)} %get-tuple-element.18) | copy-start | bytes 15728644
  49.1 2.7 %copy-start.6 = (f32[5,1024]{1,0:T(8,128)}, f32[5,1024]{1,0:T(8,128)S(1)}, u32[]{:S(2)}) copy-start(f32[5,1024]{1,0:T(8,128)S(1)} %get-tuple-element.13) | copy-start | bytes 61444
  49.2 2.7 %copy-start.8 = (f32[5,1024]{1,0:T(8,128)}, f32[5,1024]{1,0:T(8,128)S(1)}, u32[]{:S(2)}) copy-start(f32[5,1024]{1,0:T(8,128)S(1)} %get-tuple-element.14) | copy-start | bytes 61444
  49.2 10.4 %copy-start.5 = (bf16[256,640]{0,1:T(8,128)(2,1)S(1)}, bf16[256,640]{0,1:T(8,128)(2,1)}, u32[]{:S(2)}) copy-start(bf16[256,640]{0,1:T(8,128)(2,1)} %copy-done.4) | copy-start | bytes 983044
  56.3 12.4 %all-to-all-start.2 = ((f32[4,1,1280]{2,1,0:T(1,128)}), f32[4,1,1280]{2,1,0:T(1,128)S(1)}, u32[]{:S(2)}, u32[]{:S(2)}) async-start(f32[4,1,1280]{2,1,0:T(1,128)} %reshape.74), calls=%async_computation.2 | async-start | bytes 40960 | tf_op jit(solution)/shard_map/all_to_all | solution.py:93
  59.5 5.9 %copy-start.9 = (f32[1,1024,5]{1,2,0:T(8,128)S(1)}, f32[1,1024,5]{1,2,0:T(8,128)}, u32[]{:S(2)}) copy-start(f32[1,1024,5]{1,2,0:T(8,128)} %get-tuple-element.9) | copy-start | bytes 61444
  59.5 14.1 %copy-start.7 = (f32[5,1024]{1,0:T(8,128)S(1)}, f32[5,1024]{1,0:T(8,128)}, u32[]{:S(2)}) copy-start(f32[5,1024]{1,0:T(8,128)} %copy-done.6) | copy-start | bytes 61444
  59.6 14.1 %copy-start.10 = (f32[1024,5]{0,1:T(8,128)S(1)}, f32[1024,5]{0,1:T(8,128)}, u32[]{:S(2)}) copy-start(f32[1024,5]{0,1:T(8,128)} %get-tuple-element.11) | copy-start | bytes 61444
  59.6 14.1 %copy-start.11 = (f32[1024,5]{0,1:T(8,128)S(1)}, f32[1024,5]{0,1:T(8,128)}, u32[]{:S(2)}) copy-start(f32[1024,5]{0,1:T(8,128)} %get-tuple-element.12) | copy-start | bytes 61444
  68.6 14.6 %all-to-all-start = ((f32[4,1,1280]{2,1,0:T(1,128)}), f32[4,1,1280]{2,1,0:T(1,128)S(1)}, u32[]{:S(2)}, u32[]{:S(2)}) async-start(f32[4,1,1280]{2,1,0:T(1,128)} %reshape.72), calls=%async_computation | async-start | bytes 40960 | tf_op jit(solution)/shard_map/all_to_all | solution.py:92
  83.2 62.7 %all-to-all-start.1 = ((f32[1,1024,5,128]{3,0,2,1:T(1,128)}), f32[1,1024,5,128]{3,0,2,1:T(1,128)}, u32[]{:S(2)}, u32[]{:S(2)}) async-start(f32[1,1024,5,128]{3,0,2,1:T(1,128)} %copy.107), calls=%async_computation.1 | async-start | bytes 5242880 | tf_op jit(solution)/shard_map/all_to_all | solution.py:94
  88.3 97.4 %all-gather.6.cloned.1.call-start = ((), (), s32[]{:S(2)}) async-start(), calls=%async_computation.5 | async-start | bytes 1638400 | tf_op jit(solution)/shard_map/all_gather | solution.py:106
  149.9 91.7 %reduce-scatter.2.cloned.1.call-start = ((), (), s32[]{:S(2)}) async-start(), calls=%async_computation.6 | async-start | bytes 6553600 | tf_op jit(solution)/shard_map/reduce_scatter | solution.py:110
  191.6 50.1 %copy-start.12 = (f32[1280]{0:T(1024)S(1)}, f32[1280]{0:T(1024)}, u32[]{:S(2)}) copy-start(f32[1280]{0:T(1024)} %param.13) | copy-start | bytes 15364
Sparse Core Ops, SparseCore 0:
  8.9 36.2 all-gather.3
  150.0 35.6 all-gather.5
  191.7 49.8 reduce-scatter.1
where the time goes:
time: 251 us; the launch traced here: 250 us
  waiting for transfers between devices  148 us (59%)
  matrix products  20.9 us (8%)
  local copies, waits for them, and re-layouts  20.1 us (8%)
  blocking collectives  18.3 us (7%)
  starting transfers between devices  16.4 us (7%)
  between operations  14 us (6%)
  other arithmetic  13.1 us (5%)
    all_to_all x1, waiting for transfers between devices, shards(): lax.all_to_all(running_acc[None], 'rep', split_axis=1, concat_axis=0, til...  54.2 us
    reduce_scatter x1, waiting for transfers between devices, shards(): lax.psum_scatter(partial_out, 'heads', scatter_dimension=0, tiled=True)  50.1 us
    all_gather x1, waiting for transfers between devices, shards(): lax.all_gather(attended, 'rep', axis=0, tiled=True)  35.7 us
    dot_general x2, matrix products, absorb(): jnp.einsum('hqk,khd->qhd', weights.astype(jnp.bfloat16), value_part, pref...  11.2 us
    unnamed x40, local copies, waits for them, and re-layouts  10.7 us
    unnamed x1, blocking collectives  9.99 us
    all_gather x1, blocking collectives, shards(): lax.all_gather(block_lists, 'rep', axis=0, tiled=True)  8.33 us
    all_gather x1, waiting for transfers between devices, shards(): lax.all_gather(queries, 'rep', axis=0, tiled=True)  7.64 us
  transfers between devices with their start and end apart: 7, of which 4 were waited for; matrix products, arithmetic and copies ran while one was open for 12% of the time, Pallas kernels for 0%

commit v1 on v0

v1 whole, which is shorter than its diff:
```python
import functools

import jax
import jax.numpy as jnp
from jax import lax
from jax.experimental import pallas as pl
from jax.experimental.pallas import tpu as pltpu
from jax.sharding import PartitionSpec as P

HD = 128
BLOCK = 128
LIST = 16
NEG = 1e30
MESH = pl.DeviceIdType.MESH


def extra_rep(g, reps):
    half = g // 2
    return ((1 - g % 2) * half + (g % 2) * (reps - 1 - half)) % reps


def kernel(
    dims,
    q_ref, k_ref, v_ref, lists_ref, counts_ref, w_ref, gate_ref,
    out_ref,
    qbuf, kbuf, vbuf, mbuf, stage, abuf, wbuf, acc,
    zs, zr, zms, zmr, xs, xr, own_sem, w_own, ats, atr, gs, gr, wys, wyr, wms, wmr,
):
    frames, groups, reps, toks, heads, base, extra, slots, plane_heads = dims
    tm = lax.axis_index("tm")
    g = lax.axis_index("heads")
    z = lax.axis_index("rep")
    span = reps * toks
    local_blocks = toks // BLOCK
    frame_blocks = span // BLOCK
    lanes = mbuf.shape[-1]

    def cols(head):
        return pl.ds(pl.multiple_of(head * HD, HD), HD)

    def rows(rep):
        return pl.ds(pl.multiple_of(rep * toks, toks), toks)

    def extra_rank(plane, group):
        return sum(
            jnp.where((other < group) & ((plane - extra_rep(other, reps) + reps) % reps < extra), 1, 0)
            for other in range(groups)
        )

    def extra_of(group):
        return (z - extra_rep(group, reps) + reps) % reps

    my_extra = extra_of(g)
    has_extra = my_extra < extra

    def place(group, head):
        if head < base * reps:
            return head % reps, (head // reps) * groups + group
        plane = (extra_rep(group, reps) + head - base * reps) % reps
        return plane, base * groups + extra_rank(plane, group)

    barrier = pltpu.get_barrier_semaphore()
    for axis, count, me in (("rep", reps, z), ("tm", frames, tm), ("heads", groups, g)):
        for d in range(1, count):
            pl.semaphore_signal(
                barrier, inc=1, device_id={axis: (me + d) % count}, device_id_type=MESH
            )
    pl.semaphore_wait(barrier, reps + frames + groups - 3)

    row_id = lax.broadcasted_iota(jnp.int32, (8, lanes), 0)
    lane_id = lax.broadcasted_iota(jnp.int32, (8, lanes), 1)
    allowed = jnp.zeros((8, lanes), jnp.float32)
    for b in range(local_blocks):
        used = counts_ref[b]
        for j in range(LIST):
            hit = (lane_id == lists_ref[b, j]) & (row_id == b) & (jnp.full((8, lanes), j) < used)
            allowed = jnp.where(hit, 1.0, allowed)
    mbuf[z] = allowed

    def mask_copy(dst, src):
        return pltpu.make_async_remote_copy(
            src_ref=mbuf.at[src], dst_ref=mbuf.at[src],
            send_sem=zms.at[dst], recv_sem=zmr.at[src],
            device_id={"rep": dst}, device_id_type=MESH,
        )

    sources = (k_ref, v_ref, q_ref)

    def landing(kind, slot, rep):
        if kind == 2:
            return qbuf.at[slot, rows(rep)]
        return (kbuf, vbuf)[kind].at[slot, tm, rows(rep)]

    def z_copy(kind, slot, head, dst, src):
        return pltpu.make_async_remote_copy(
            src_ref=sources[kind].at[:, cols(head)], dst_ref=landing(kind, slot, src),
            send_sem=zs.at[kind, slot, dst], recv_sem=zr.at[kind, slot, src],
            device_id={"rep": dst}, device_id_type=MESH,
        )

    def own_copy(kind, slot, head):
        return pltpu.make_async_copy(
            sources[kind].at[:, cols(head)], landing(kind, slot, z), own_sem.at[kind, slot]
        )

    def x_copy(kind, slot, rep, d, src=None):
        there = landing(kind, slot, rep)
        return pltpu.make_async_remote_copy(
            src_ref=there if src is None else src, dst_ref=there,
            send_sem=xs.at[kind, slot, rep, d - 1], recv_sem=xr.at[kind, slot, rep, d - 1],
            device_id={"tm": (tm + d) % frames}, device_id_type=MESH,
        )

    def my_head(slot):
        return slot * reps + z if slot < base else base * reps + my_extra

    def each_slot(act):
        for slot in range(base):
            act(slot)
        if extra:
            pl.when(has_extra)(lambda: act(base))

    for d in range(1, reps):
        mask_copy((z + d) % reps, z).start()
    for kind in range(3):
        for d in range(1, reps):
            dst = (z + d) % reps
            for slot in range(base):
                z_copy(kind, slot, slot * reps + dst, dst, z).start()
        for n in range(extra):
            dst = (extra_rep(g, reps) + n) % reps

            @pl.when(dst != z)
            def _():
                z_copy(kind, base, base * reps + n, dst, z).start()

        def start_own(slot):
            own_copy(kind, slot, my_head(slot)).start()
            if kind < 2:
                for d in range(1, frames):
                    x_copy(kind, slot, z, d, sources[kind].at[:, cols(my_head(slot))]).start()

        each_slot(start_own)

    mate = g + 1 - 2 * (g % 2)

    def w_there(group, head):
        plane, at = place(group, head)
        return wbuf.at[plane, cols(at)]

    def w_far(k, head):
        return pltpu.make_async_remote_copy(
            src_ref=w_ref.at[pl.ds(head * HD, HD)], dst_ref=w_there(g, head),
            send_sem=wys.at[k - 1, head], recv_sem=wyr.at[k - 1, head],
            device_id={"heads": (g + 2 * k) % groups}, device_id_type=MESH,
        )

    def w_mate(k, head):
        from_group = (g - 2 * k + groups) % groups
        there = w_there(from_group, head)
        return pltpu.make_async_remote_copy(
            src_ref=there if k else w_ref.at[pl.ds(head * HD, HD)], dst_ref=there,
            send_sem=wms.at[k, head], recv_sem=wmr.at[k, head],
            device_id={"heads": mate}, device_id_type=MESH,
        )

    def w_local(head):
        return pltpu.make_async_copy(
            w_ref.at[pl.ds(head * HD, HD)], w_there(g, head), w_own.at[head]
        )

    halves = groups // 2
    for head in range(heads):
        for k in range(1, halves):
            w_far(k, head).start()
    for head in range(heads):
        w_mate(0, head).start()
        w_local(head).start()

    for kind in range(2):
        for d in range(1, reps):
            src = (z + d) % reps

            def pass_on(slot):
                z_copy(kind, slot, 0, z, src).wait_recv()
                for e in range(1, frames):
                    x_copy(kind, slot, src, e).start()

            each_slot(pass_on)
    for d in range(1, reps):
        mask_copy(z, (z + d) % reps).wait_recv()

    def rest(slot):
        for kind in range(3):
            own_copy(kind, slot, my_head(slot)).wait()
        for kind in range(2):
            for rep in range(reps):
                for d in range(1, frames):
                    there = (kbuf, vbuf)[kind].at[slot, (tm - d + frames) % frames, rows(rep)]
                    pltpu.make_async_remote_copy(
                        src_ref=there, dst_ref=there,
                        send_sem=xs.at[kind, slot, rep, d - 1],
                        recv_sem=xr.at[kind, slot, rep, d - 1],
                        device_id={"tm": (tm + d) % frames}, device_id_type=MESH,
                    ).wait_recv()

    each_slot(rest)

    def attend(slot, chunk):
        queries = qbuf[slot, rows(chunk)]
        mask_rows = mbuf[chunk].astype(jnp.bfloat16)
        block_of = lax.broadcasted_iota(jnp.int32, (lanes, span), 1) // BLOCK
        lane_of = lax.broadcasted_iota(jnp.int32, (lanes, span), 0)
        factor = 1.4426950408889634 / HD**0.5

        def step(frame, state):
            top, total, sums = state
            spread = jnp.where(block_of + frame * frame_blocks == lane_of, 1.0, 0.0)
            bias = NEG * (
                jnp.dot(mask_rows, spread.astype(jnp.bfloat16), preferred_element_type=jnp.float32)
                - 1.0
            )
            scores = lax.dot_general(
                queries, kbuf[slot, frame], (((1,), (1,)), ((), ())),
                preferred_element_type=jnp.float32,
            )
            scores = scores + jnp.concatenate(
                [jnp.broadcast_to(bias[b : b + 1], (BLOCK, span)) for b in range(local_blocks)], 0
            )
            new_top = jnp.maximum(top, jnp.max(scores, axis=1, keepdims=True))
            weights = jnp.exp2((scores - new_top) * factor)
            scale = jnp.exp2((top - new_top) * factor)
            total = total * scale + jnp.sum(weights, axis=1, keepdims=True)
            sums = sums * scale + jnp.dot(
                weights.astype(jnp.bfloat16), vbuf[slot, frame], preferred_element_type=jnp.float32
            )
            return new_top, total, sums

        state = (
            jnp.full((toks, 1), -NEG, jnp.float32),
            jnp.zeros((toks, 1), jnp.float32),
            jnp.zeros((toks, HD), jnp.float32),
        )
        _, total, sums = lax.fori_loop(0, frames, step, state, unroll=min(frames, 2))
        stage[slot, rows(chunk)] = (sums / total).astype(jnp.bfloat16)

    def position(slot, group):
        return slot * groups + group if slot < base else base * groups + extra_rank(z, group)

    def att_copy(slot, chunk):
        return pltpu.make_async_remote_copy(
            src_ref=stage.at[slot, rows(chunk)], dst_ref=abuf.at[z, :, cols(position(slot, g))],
            send_sem=ats.at[slot, chunk], recv_sem=atr.at[slot, g],
            device_id={"heads": chunk}, device_id_type=MESH,
        )

    def att_local(slot):
        return pltpu.make_async_copy(
            stage.at[slot, rows(g)], abuf.at[z, :, cols(position(slot, g))], ats.at[slot, g]
        )

    def one_chunk(i, _):
        chunk = (z + i) % reps

        def work(slot):
            @pl.when(i > 0)
            def _():
                z_copy(2, slot, 0, z, chunk).wait_recv()

            attend(slot, chunk)

            @pl.when(chunk != g)
            def _():
                att_copy(slot, chunk).start()

            @pl.when(chunk == g)
            def _():
                att_local(slot).start()

        each_slot(work)
        return 0

    lax.fori_loop(0, reps, one_chunk, 0)

    each_slot(lambda slot: att_local(slot).wait())
    for d in range(1, groups):
        other = (g + d) % groups

        def arrive(slot):
            there = abuf.at[z, :, cols(position(slot, other))]
            pltpu.make_async_remote_copy(
                src_ref=stage.at[slot, rows(g)], dst_ref=there,
                send_sem=ats.at[slot, other], recv_sem=atr.at[slot, other],
                device_id={"heads": other}, device_id_type=MESH,
            ).wait_recv()

        for slot in range(base):
            arrive(slot)
        if extra:
            pl.when(extra_of(other) < extra)(lambda: arrive(base))

    def line_copy(src, way):
        return pltpu.make_async_remote_copy(
            src_ref=abuf.at[src], dst_ref=abuf.at[src],
            send_sem=gs.at[(way + 1) // 2, src], recv_sem=gr.at[src],
            device_id={"rep": (z + way + reps) % reps}, device_id_type=MESH,
        )

    @pl.when(z + 1 < reps)
    def _():
        line_copy(z, 1).start()

    @pl.when(z > 0)
    def _():
        line_copy(z, -1).start()

    for head in range(heads):
        for k in range(1, halves):
            w_far(k, head).wait_recv()
            w_mate(k, head).start()
    for head in range(heads):
        for k in range(halves):
            w_mate(k, head).wait_recv()
        w_local(head).wait()

    def product(src):
        return jnp.dot(abuf[src], wbuf[src], preferred_element_type=jnp.float32)

    acc[...] = product(z)
    for d in range(1, reps):
        @pl.when(z - d >= 0)
        def _():
            src = (z - d + reps) % reps
            line_copy(src, 1).wait_recv()

            @pl.when(z + 1 < reps)
            def _():
                line_copy(src, 1).start()

        @pl.when(z + d < reps)
        def _():
            src = (z + d) % reps
            line_copy(src, -1).wait_recv()

            @pl.when(z > 0)
            def _():
                line_copy(src, -1).start()

        @pl.when(z - d >= 0)
        def _():
            acc[...] += product((z - d + reps) % reps)

        @pl.when(z + d < reps)
        def _():
            acc[...] += product((z + d) % reps)

    out_ref[...] = (gate_ref[...] * acc[...]).astype(out_ref.dtype)

    for d in range(1, reps):
        dst = (z + d) % reps
        mask_copy(dst, z).wait_send()
        for kind in range(3):
            for slot in range(base):
                z_copy(kind, slot, slot * reps + dst, dst, z).wait_send()
    for n in range(extra):
        dst = (extra_rep(g, reps) + n) % reps

        @pl.when(dst != z)
        def _():
            for kind in range(3):
                z_copy(kind, base, base * reps + n, dst, z).wait_send()

    def sent(slot):
        for kind in range(2):
            for rep in range(reps):
                for d in range(1, frames):
                    x_copy(kind, slot, rep, d).wait_send()
        for d in range(1, groups):
            att_copy(slot, (g + d) % groups).wait_send()

    each_slot(sent)
    for head in range(heads):
        for k in range(1, halves):
            w_far(k, head).wait_send()
        for k in range(halves):
            w_mate(k, head).wait_send()

    @pl.when(z + 1 < reps)
    def _():
        for src in range(reps):
            pl.when(src <= z)(lambda: line_copy(src, 1).wait_send())

    @pl.when(z > 0)
    def _():
        for src in range(reps):
            pl.when(src >= z)(lambda: line_copy(src, -1).wait_send())


def shards(queries, keys, values, block_lists, list_counts, out_weight, gate):
    frames, groups, reps = (lax.axis_size(a) for a in ("tm", "heads", "rep"))
    toks = queries.shape[0]
    heads = queries.shape[1] // HD
    wide = out_weight.shape[1]
    base, extra = heads // reps, heads % reps
    slots = base + (1 if extra else 0)
    assert groups == reps and groups % 2 == 0
    plane_heads = heads * groups // reps
    span = reps * toks
    lanes = -(-(span * frames // BLOCK) // 128) * 128
    dims = (frames, groups, reps, toks, heads, base, extra, slots, plane_heads)
    others = max(frames - 1, 1)
    halves = groups // 2
    vmem, smem, hbm = (
        pl.BlockSpec(memory_space=m) for m in (pltpu.VMEM, pltpu.SMEM, pl.ANY)
    )
    dma = pltpu.SemaphoreType.DMA
    scores = slots * span * span * frames
    return pl.pallas_call(
        functools.partial(kernel, dims),
        out_shape=jax.ShapeDtypeStruct((toks, wide), jnp.bfloat16),
        in_specs=[hbm, hbm, hbm, smem, smem, hbm, vmem],
        out_specs=vmem,
        scratch_shapes=[
            pltpu.VMEM((slots, span, HD), jnp.bfloat16),
            pltpu.VMEM((slots, frames, span, HD), jnp.bfloat16),
            pltpu.VMEM((slots, frames, span, HD), jnp.bfloat16),
            pltpu.VMEM((reps, 8, lanes), jnp.float32),
            pltpu.VMEM((slots, span, HD), jnp.bfloat16),
            pltpu.VMEM((reps, toks, plane_heads * HD), jnp.bfloat16),
            pltpu.VMEM((reps, plane_heads * HD, wide), jnp.bfloat16),
            pltpu.VMEM((toks, wide), jnp.float32),
            dma((3, slots, reps)), dma((3, slots, reps)),
            dma((reps,)), dma((reps,)),
            dma((2, slots, reps, others)), dma((2, slots, reps, others)),
            dma((3, slots)), dma((heads,)),
            dma((slots, groups)), dma((slots, groups)),
            dma((2, reps)), dma((reps,)),
            dma((max(halves - 1, 1), heads)), dma((max(halves - 1, 1), heads)),
            dma((halves, heads)), dma((halves, heads)),
        ],
        compiler_params=pltpu.CompilerParams(
            collective_id=0, has_side_effects=True, vmem_limit_bytes=56 * 2**20
        ),
        cost_estimate=pl.CostEstimate(
            flops=4 * scores * HD + 2 * toks * plane_heads * HD * reps * wide,
            bytes_accessed=2 * (3 * queries.size + out_weight.size),
            transcendentals=scores,
        ),
    )(queries, keys, values, block_lists, list_counts, out_weight, gate.reshape(1, wide))


def solution(mesh):
    placed = (
        P(("tm", "rep"), "heads"),
        P(("tm", "rep"), "heads"),
        P(("tm", "rep"), "heads"),
        P(("tm", "rep"), None),
        P(("tm", "rep")),
        P("heads", "rep"),
        P("rep"),
    )
    return jax.shard_map(
        shards, mesh=mesh, in_specs=placed, out_specs=P(("tm", "heads"), "rep"), check_vma=False
    )
```

time: 251 us -> 78.1 us (0.31)
  waiting for transfers between devices: 148 us -> 0 us
  Pallas kernels: 0 us -> 74.6 us
  matrix products: 20.9 us -> 0 us
  blocking collectives: 18.3 us -> 0 us
  local copies, waits for them, and re-layouts: 20.1 us -> 3.26 us
  starting transfers between devices: 16.4 us -> 0 us
  between operations: 14 us -> 0.01 us
  other arithmetic: 13.1 us -> 0 us
    pallas_call x0 -> x1, Pallas kernels: none -> 74.6 us  [shards(): pl.pallas_call(functools.partial(kernel, dims), out_shape=jax.ShapeDtypeS...]
    all_to_all x3 -> x0, waiting for transfers between devices: 54.3 us -> none  [the longest x1 54.2 us: shards(): lax.all_to_all(running_acc[None], 'rep', split_axis=1, concat_axis=0, til...]
    reduce_scatter x1 -> x0, waiting for transfers between devices: 50.1 us -> none  [shards(): lax.psum_scatter(partial_out, 'heads', scatter_dimension=0, tiled=True)]
    all_gather x2 -> x0, waiting for transfers between devices: 43.4 us -> none  [the longest x1 35.7 us: shards(): lax.all_gather(attended, 'rep', axis=0, tiled=True)]
    dot_general x5 -> x0, matrix products: 20.9 us -> none  [the longest x2 11.2 us: absorb(): jnp.einsum('hqk,khd->qhd', weights.astype(jnp.bfloat16), value_part, pref...]
    all_to_all x3 -> x0, starting transfers between devices: 13.4 us -> none  [the longest x1 5.08 us: shards(): lax.all_to_all(running_acc[None], 'rep', split_axis=1, concat_axis=0, til...]
    unnamed x1 -> x0, blocking collectives: 9.99 us -> none
    unnamed x40 -> x1, local copies, waits for them, and re-layouts: 10.7 us -> 1.97 us
  transfers between devices with their start and end apart: 7 -> 0, of which waited for: 4 -> 0; matrix products, arithmetic and copies ran while one was open for 12% -> 0% of each run, Pallas kernels for 0% -> 0%
where the time goes in v1:
time: 78.1 us; the launch traced here: 77.8 us
  Pallas kernels  74.6 us (96%)
  local copies, waits for them, and re-layouts  3.26 us (4%)
    pallas_call x1, Pallas kernels, shards(): pl.pallas_call(functools.partial(kernel, dims), out_shape=jax.ShapeDtypeS...  74.6 us
    unnamed x1, local copies, waits for them, and re-layouts  1.97 us

profile of v1, /device:TPU:0, one launch (start us, length us, event | category | flops | bytes accessed | tf_op | source)
XLA Modules:
  0.0 77.8 jit_solution(1790296693574485570)
XLA Ops:
  0.0 1.3 %reshape.3.gate_ref = f32[1,1280]{1,0:T(1,128)} reshape(f32[1280]{0:T(1024)} %param.13) | data formatting | bytes 10240 | tf_op jit(solution)/shard_map/reshape | solution.py:449
  1.3 74.6 %shard_map.73 = bf16[256,1280]{1,0:T(8,128)(2,1)} custom-call(bf16[256,640]{1,0:T(8,128)(2,1)} %q_ref.1, bf16[256,640]{1,0:T(8,128)(2,1)} %k_ref.1, bf16[256,640]{1,0:T(8,128)(2,1)} %v_ref.1, s32[2,16]{1,0:T(2,128)} %lists_ref.1, s32[2]{0:T(128)} %counts_ref.1, bf16[640,1280]{1,0:T(8,128)(2,1)} %w_ref.1, f32[1,1280]{1,0:T(1,128)} %reshape.3.gate_ref), custom_call_target="tpu_custom_call" | custom-call | flops 3825205248 | bytes 2621440 | tf_op jit(solution)/shard_map/pallas_call | solution.py:418
  75.9 2.0 %copy.9 = bf16[256,1280]{1,0:T(8,128)(2,1)} copy(bf16[256,1280]{1,0:T(8,128)(2,1)} %shard_map.73) | data formatting | bytes 1310720

commit v2 on v1

v2 whole, which is shorter than its diff:
```python
import functools

import jax
import jax.numpy as jnp
from jax import lax
from jax.experimental import pallas as pl
from jax.experimental.pallas import tpu as pltpu
from jax.sharding import PartitionSpec as P

HD = 128
BLOCK = 128
LIST = 16
NEG = 1e30
MESH = pl.DeviceIdType.MESH


def extra_rep(g, reps):
    half = g // 2
    return ((1 - g % 2) * half + (g % 2) * (reps - 1 - half)) % reps


def kernel(
    dims,
    q_ref, k_ref, v_ref, lists_ref, counts_ref, w_ref,
    out_ref,
    qbuf, kbuf, vbuf, mbuf, bias_buf, stage, abuf, wbuf,
    zs, zr, zms, zmr, xs, xr, own_sem, w_own, ats, atr, gs, gr, wys, wyr, wxs, wxr, wms, wmr,
):
    frames, groups, reps, toks, heads, base, extra, parts = dims
    tm = lax.axis_index("tm")
    g = lax.axis_index("heads")
    z = lax.axis_index("rep")
    span = reps * toks
    local_blocks = toks // BLOCK
    frame_blocks = span // BLOCK
    lanes = mbuf.shape[-1]
    part_cols = w_ref.shape[1] // parts
    halves = groups // 2

    def cols(head):
        return pl.ds(pl.multiple_of(head * HD, HD), HD)

    def rows(rep):
        return pl.ds(pl.multiple_of(rep * toks, toks), toks)

    def extra_rank(plane, group):
        return sum(
            jnp.where((other < group) & ((plane - extra_rep(other, reps) + reps) % reps < extra), 1, 0)
            for other in range(groups)
        )

    def extra_of(group):
        return (z - extra_rep(group, reps) + reps) % reps

    my_extra = extra_of(g)
    has_extra = my_extra < extra

    def place(group, head):
        if head < base * reps:
            return head % reps, (head // reps) * groups + group
        plane = (extra_rep(group, reps) + head - base * reps) % reps
        return plane, base * groups + extra_rank(plane, group)

    barrier = pltpu.get_barrier_semaphore()
    for axis, count, me in (("rep", reps, z), ("tm", frames, tm), ("heads", groups, g)):
        for d in range(1, count):
            pl.semaphore_signal(
                barrier, inc=1, device_id={axis: (me + d) % count}, device_id_type=MESH
            )
    pl.semaphore_wait(barrier, reps + frames + groups - 3)

    def mask_copy(dst, src):
        return pltpu.make_async_remote_copy(
            src_ref=mbuf.at[src], dst_ref=mbuf.at[src],
            send_sem=zms.at[dst], recv_sem=zmr.at[src],
            device_id={"rep": dst}, device_id_type=MESH,
        )

    sources = (k_ref, v_ref, q_ref)

    def landing(kind, slot, rep):
        if kind == 2:
            return qbuf.at[slot, rows(rep)]
        return (kbuf, vbuf)[kind].at[slot, tm, rows(rep)]

    def z_copy(kind, slot, head, dst, src):
        return pltpu.make_async_remote_copy(
            src_ref=sources[kind].at[:, cols(head)], dst_ref=landing(kind, slot, src),
            send_sem=zs.at[kind, slot, dst], recv_sem=zr.at[kind, slot, src],
            device_id={"rep": dst}, device_id_type=MESH,
        )

    def own_copy(kind, slot, head):
        return pltpu.make_async_copy(
            sources[kind].at[:, cols(head)], landing(kind, slot, z), own_sem.at[kind, slot]
        )

    def x_copy(kind, slot, rep, d, src=None):
        there = landing(kind, slot, rep)
        return pltpu.make_async_remote_copy(
            src_ref=there if src is None else src, dst_ref=there,
            send_sem=xs.at[kind, slot, rep, d - 1], recv_sem=xr.at[kind, slot, rep, d - 1],
            device_id={"tm": (tm + d) % frames}, device_id_type=MESH,
        )

    def my_head(slot):
        return slot * reps + z if slot < base else base * reps + my_extra

    def if_extra(act):
        if extra:
            pl.when(has_extra)(lambda: act(base))

    def each_base(act):
        for slot in range(base):
            act(slot)

    def start_own(kind, slot):
        if kind < 2:
            for d in range(1, frames):
                x_copy(kind, slot, z, d, sources[kind].at[:, cols(my_head(slot))]).start()
        own_copy(kind, slot, my_head(slot)).start()

    for kind in range(3):
        for d in range(1, reps):
            dst = (z + d) % reps
            each_base(lambda slot: z_copy(kind, slot, slot * reps + dst, dst, z).start())
        each_base(lambda slot: start_own(kind, slot))

    mate = g + 1 - 2 * (g % 2)
    pieces = heads * parts

    def w_here(piece):
        return w_ref.at[
            pl.ds(piece // parts * HD, HD), pl.ds(piece % parts * part_cols, part_cols)
        ]

    def w_there(group, piece):
        plane, at = place(group, piece // parts)
        return wbuf.at[plane, cols(at), pl.ds(piece % parts * part_cols, part_cols)]

    def w_far(k, piece):
        return pltpu.make_async_remote_copy(
            src_ref=w_here(piece), dst_ref=w_there(g, piece),
            send_sem=wys.at[k - 1, piece], recv_sem=wyr.at[k - 1, piece],
            device_id={"heads": (g + 2 * k) % groups}, device_id_type=MESH,
        )

    def w_frame(k, piece, d):
        there = w_there((g - 2 * k + groups) % groups, piece)
        return pltpu.make_async_remote_copy(
            src_ref=there, dst_ref=there,
            send_sem=wxs.at[k - 1, piece, d - 1], recv_sem=wxr.at[k - 1, piece],
            device_id={"tm": (tm + d) % frames}, device_id_type=MESH,
        )

    def w_mate(k, piece):
        there = w_there((g - 2 * k + groups) % groups, piece)
        return pltpu.make_async_remote_copy(
            src_ref=there if k else w_here(piece), dst_ref=there,
            send_sem=wms.at[k, piece], recv_sem=wmr.at[k, piece],
            device_id={"heads": mate}, device_id_type=MESH,
        )

    def w_local(piece):
        return pltpu.make_async_copy(w_here(piece), w_there(g, piece), w_own.at[piece])

    def w_share(act, mine=True):
        for piece in range(pieces):
            fetch = tm == piece % frames

            @pl.when(fetch if mine else jnp.logical_not(fetch))
            def _():
                for k in range(1, halves):
                    act(k, piece)

    w_share(lambda k, piece: w_far(k, piece).start())

    row_id = lax.broadcasted_iota(jnp.int32, (8, lanes), 0)
    lane_id = lax.broadcasted_iota(jnp.int32, (8, lanes), 1)
    allowed = jnp.zeros((8, lanes), jnp.float32)
    for b in range(local_blocks):
        used = counts_ref[b]
        for j in range(LIST):
            hit = (lane_id == lists_ref[b, j]) & (row_id == b) & (jnp.full((8, lanes), j) < used)
            allowed = jnp.where(hit, 1.0, allowed)
    mbuf[z] = allowed
    for d in range(1, reps):
        mask_copy((z + d) % reps, z).start()

    for kind in range(3):
        for n in range(extra):
            dst = (extra_rep(g, reps) + n) % reps

            @pl.when(dst != z)
            def _():
                z_copy(kind, base, base * reps + n, dst, z).start()

        if_extra(lambda slot: start_own(kind, slot))

    for piece in range(pieces):
        w_mate(0, piece).start()
        w_local(piece).start()

    for d in range(1, reps):
        mask_copy(z, (z + d) % reps).wait_recv()
    mask_rows = mbuf[...].reshape(reps * 8, lanes).astype(jnp.bfloat16)
    block_of = lax.broadcasted_iota(jnp.int32, (lanes, span), 1) // BLOCK
    lane_of = lax.broadcasted_iota(jnp.int32, (lanes, span), 0)

    def spread_mask(frame, _):
        spread = jnp.where(block_of + frame * frame_blocks == lane_of, 1.0, 0.0)
        hits = jnp.dot(
            mask_rows, spread.astype(jnp.bfloat16), preferred_element_type=jnp.float32
        )
        bias_buf[frame] = (NEG * (hits - 1.0)).reshape(reps, 8, span)
        return 0

    lax.fori_loop(0, frames, spread_mask, 0)

    def pass_on(slot):
        for kind in range(2):
            for d in range(1, reps):
                src = (z + d) % reps
                z_copy(kind, slot, 0, z, src).wait_recv()
                for e in range(1, frames):
                    x_copy(kind, slot, src, e).start()

    def rest(slot):
        for kind in range(3):
            own_copy(kind, slot, my_head(slot)).wait()
        for kind in range(2):
            for rep in range(reps):
                for d in range(1, frames):
                    there = (kbuf, vbuf)[kind].at[slot, (tm - d + frames) % frames, rows(rep)]
                    pltpu.make_async_remote_copy(
                        src_ref=there, dst_ref=there,
                        send_sem=xs.at[kind, slot, rep, d - 1],
                        recv_sem=xr.at[kind, slot, rep, d - 1],
                        device_id={"tm": (tm + d) % frames}, device_id_type=MESH,
                    ).wait_recv()

    def attend(slot, chunk):
        queries = qbuf[slot, rows(chunk)]
        factor = 1.4426950408889634 / HD**0.5

        def step(frame, state):
            top, total, sums = state
            bias = bias_buf[frame, chunk]
            scores = lax.dot_general(
                queries, kbuf[slot, frame], (((1,), (1,)), ((), ())),
                preferred_element_type=jnp.float32,
            )
            scores = scores + jnp.concatenate(
                [jnp.broadcast_to(bias[b : b + 1], (BLOCK, span)) for b in range(local_blocks)], 0
            )
            new_top = jnp.maximum(top, jnp.max(scores, axis=1, keepdims=True))
            weights = jnp.exp2((scores - new_top) * factor)
            scale = jnp.exp2((top - new_top) * factor)
            total = total * scale + jnp.sum(weights, axis=1, keepdims=True)
            sums = sums * scale + jnp.dot(
                weights.astype(jnp.bfloat16), vbuf[slot, frame], preferred_element_type=jnp.float32
            )
            return new_top, total, sums

        state = (
            jnp.full((toks, 1), -NEG, jnp.float32),
            jnp.zeros((toks, 1), jnp.float32),
            jnp.zeros((toks, HD), jnp.float32),
        )
        _, total, sums = lax.fori_loop(0, frames, step, state, unroll=min(frames, 2))
        stage[slot, rows(chunk)] = (sums / total).astype(jnp.bfloat16)

    def position(slot, group):
        return slot * groups + group if slot < base else base * groups + extra_rank(z, group)

    def att_copy(slot, chunk):
        return pltpu.make_async_remote_copy(
            src_ref=stage.at[slot, rows(chunk)], dst_ref=abuf.at[z, :, cols(position(slot, g))],
            send_sem=ats.at[slot, chunk], recv_sem=atr.at[slot, g],
            device_id={"heads": chunk}, device_id_type=MESH,
        )

    def att_local(slot):
        return pltpu.make_async_copy(
            stage.at[slot, rows(g)], abuf.at[z, :, cols(position(slot, g))], ats.at[slot, g]
        )

    def arrive(slot, other):
        there = abuf.at[z, :, cols(position(slot, other))]
        pltpu.make_async_remote_copy(
            src_ref=stage.at[slot, rows(g)], dst_ref=there,
            send_sem=ats.at[slot, other], recv_sem=atr.at[slot, other],
            device_id={"heads": other}, device_id_type=MESH,
        ).wait_recv()

    def attend_all(slot):
        def one_chunk(i, _):
            chunk = (z + i) % reps

            @pl.when(i > 0)
            def _():
                z_copy(2, slot, 0, z, chunk).wait_recv()

            attend(slot, chunk)

            @pl.when(chunk != g)
            def _():
                att_copy(slot, chunk).start()

            @pl.when(chunk == g)
            def _():
                att_local(slot).start()

            return 0

        lax.fori_loop(0, reps, one_chunk, 0)

    line_cols = (pl.ds(0, base * groups * HD), pl.ds(base * groups * HD, (heads - base * reps) * HD))
    line_parts = 2 if extra else 1

    def line_copy(part, src, way):
        there = abuf.at[src, :, line_cols[part]]
        return pltpu.make_async_remote_copy(
            src_ref=there, dst_ref=there,
            send_sem=gs.at[part, (way + 1) // 2, src], recv_sem=gr.at[part, src],
            device_id={"rep": (z + way + reps) % reps}, device_id_type=MESH,
        )

    def line_start(part):
        @pl.when(z + 1 < reps)
        def _():
            line_copy(part, z, 1).start()

        @pl.when(z > 0)
        def _():
            line_copy(part, z, -1).start()

    def line_relay(part, d):
        @pl.when(z - d >= 0)
        def _():
            src = (z - d + reps) % reps
            line_copy(part, src, 1).wait_recv()

            @pl.when(z + 1 < reps)
            def _():
                line_copy(part, src, 1).start()

        @pl.when(z + d < reps)
        def _():
            src = (z + d) % reps
            line_copy(part, src, -1).wait_recv()

            @pl.when(z > 0)
            def _():
                line_copy(part, src, -1).start()

    each_base(pass_on)
    each_base(rest)
    each_base(attend_all)
    if_extra(pass_on)

    def send_on(k, piece):
        w_far(k, piece).wait_recv()
        for d in range(1, frames):
            w_frame(k, piece, d).start()
        w_mate(k, piece).start()

    w_share(send_on)
    each_base(lambda slot: att_local(slot).wait())
    for d in range(1, groups):
        each_base(lambda slot: arrive(slot, (g + d) % groups))
    line_start(0)

    if_extra(rest)
    if_extra(attend_all)
    for d in range(1, reps - 1):
        line_relay(0, d)
        if d == 1 and extra:
            if_extra(lambda slot: att_local(slot).wait())
            for e in range(1, groups):
                other = (g + e) % groups
                pl.when(extra_of(other) < extra)(lambda: arrive(base, other))
            line_start(1)
    if extra:
        for d in range(1, reps - 1):
            line_relay(1, d)

    def to_mate(k, piece):
        w_frame(k, piece, 1).wait_recv()
        w_mate(k, piece).start()

    w_share(to_mate, mine=False)
    for piece in range(pieces):
        for k in range(halves):
            w_mate(k, piece).wait_recv()
        w_local(piece).wait()

    def product(src):
        return jnp.dot(abuf[src], wbuf[src], preferred_element_type=jnp.float32)

    out_ref[...] = product(z)
    for d in range(1, reps):
        if d == reps - 1:
            for part in range(line_parts):
                line_relay(part, d)

        @pl.when(z - d >= 0)
        def _():
            out_ref[...] += product((z - d + reps) % reps)

        @pl.when(z + d < reps)
        def _():
            out_ref[...] += product((z + d) % reps)

    for d in range(1, reps):
        dst = (z + d) % reps
        mask_copy(dst, z).wait_send()
        for kind in range(3):
            each_base(lambda slot: z_copy(kind, slot, slot * reps + dst, dst, z).wait_send())
    for n in range(extra):
        dst = (extra_rep(g, reps) + n) % reps

        @pl.when(dst != z)
        def _():
            for kind in range(3):
                z_copy(kind, base, base * reps + n, dst, z).wait_send()

    def sent(slot):
        for kind in range(2):
            for rep in range(reps):
                for d in range(1, frames):
                    x_copy(kind, slot, rep, d).wait_send()
        for d in range(1, groups):
            att_copy(slot, (g + d) % groups).wait_send()

    each_base(sent)
    if_extra(sent)

    def share_sent(k, piece):
        w_far(k, piece).wait_send()
        for d in range(1, frames):
            w_frame(k, piece, d).wait_send()

    w_share(share_sent)
    for piece in range(pieces):
        for k in range(halves):
            w_mate(k, piece).wait_send()

    for part in range(line_parts):
        @pl.when(z + 1 < reps)
        def _():
            for src in range(reps):
                pl.when(src <= z)(lambda: line_copy(part, src, 1).wait_send())

        @pl.when(z > 0)
        def _():
            for src in range(reps):
                pl.when(src >= z)(lambda: line_copy(part, src, -1).wait_send())


def shards(queries, keys, values, block_lists, list_counts, out_weight, gate):
    frames, groups, reps = (lax.axis_size(a) for a in ("tm", "heads", "rep"))
    toks = queries.shape[0]
    heads = queries.shape[1] // HD
    wide = out_weight.shape[1]
    base, extra = heads // reps, heads % reps
    slots = base + (1 if extra else 0)
    assert groups == reps and groups % 2 == 0
    plane_heads = heads * groups // reps
    span = reps * toks
    lanes = -(-(span * frames // BLOCK) // 128) * 128
    parts = 2 if wide % 256 == 0 else 1
    dims = (frames, groups, reps, toks, heads, base, extra, parts)
    others = max(frames - 1, 1)
    halves = groups // 2
    far = max(halves - 1, 1)
    pieces = heads * parts
    vmem, smem, hbm = (
        pl.BlockSpec(memory_space=m) for m in (pltpu.VMEM, pltpu.SMEM, pl.ANY)
    )
    dma = pltpu.SemaphoreType.DMA
    scores = slots * span * span * frames
    summed = pl.pallas_call(
        functools.partial(kernel, dims),
        out_shape=jax.ShapeDtypeStruct((toks, wide), jnp.float32),
        in_specs=[hbm, hbm, hbm, smem, smem, hbm],
        out_specs=vmem,
        scratch_shapes=[
            pltpu.VMEM((slots, span, HD), jnp.bfloat16),
            pltpu.VMEM((slots, frames, span, HD), jnp.bfloat16),
            pltpu.VMEM((slots, frames, span, HD), jnp.bfloat16),
            pltpu.VMEM((reps, 8, lanes), jnp.float32),
            pltpu.VMEM((frames, reps, 8, span), jnp.float32),
            pltpu.VMEM((slots, span, HD), jnp.bfloat16),
            pltpu.VMEM((reps, toks, plane_heads * HD), jnp.bfloat16),
            pltpu.VMEM((reps, plane_heads * HD, wide), jnp.bfloat16),
            dma((3, slots, reps)), dma((3, slots, reps)),
            dma((reps,)), dma((reps,)),
            dma((2, slots, reps, others)), dma((2, slots, reps, others)),
            dma((3, slots)), dma((pieces,)),
            dma((slots, groups)), dma((slots, groups)),
            dma((2, 2, reps)), dma((2, reps)),
            dma((far, pieces)), dma((far, pieces)),
            dma((far, pieces, others)), dma((far, pieces)),
            dma((halves, pieces)), dma((halves, pieces)),
        ],
        compiler_params=pltpu.CompilerParams(
            collective_id=0, has_side_effects=True, vmem_limit_bytes=56 * 2**20
        ),
        cost_estimate=pl.CostEstimate(
            flops=4 * scores * HD + 2 * toks * plane_heads * HD * reps * wide,
            bytes_accessed=2 * (3 * queries.size + out_weight.size),
            transcendentals=scores,
        ),
    )(queries, keys, values, block_lists, list_counts, out_weight)
    return (gate[None, :] * summed).astype(jnp.bfloat16)


def solution(mesh):
    placed = (
        P(("tm", "rep"), "heads"),
        P(("tm", "rep"), "heads"),
        P(("tm", "rep"), "heads"),
        P(("tm", "rep"), None),
        P(("tm", "rep")),
        P("heads", "rep"),
        P("rep"),
    )
    return jax.shard_map(
        shards, mesh=mesh, in_specs=placed, out_specs=P(("tm", "heads"), "rep"), check_vma=False
    )
```

time: 78.1 us -> 79.7 us (1.020)
  the two profiles are of different devices: /device:TPU:0 before, /device:TPU:7 now
where the time goes in v2:
time: 79.7 us; the launch traced here: 79.5 us
  Pallas kernels  77.2 us (97%)
  other arithmetic  2.23 us (3%)
    pallas_call x1, Pallas kernels, shards(): pl.pallas_call(functools.partial(kernel, dims), out_shape=jax.ShapeDtypeS...  77.2 us
    convert_element_type x1, other arithmetic, shards(): return (gate[None, :] * summed).astype(jnp.bfloat16)  2.23 us

profile of v2, /device:TPU:7, one launch (start us, length us, event | category | flops | bytes accessed | tf_op | source)
XLA Modules:
  0.0 79.5 jit_solution(5128254292868626176)
XLA Ops:
  0.0 0.0 copy-start
  0.0 77.2 %shard_map.73 = f32[256,1280]{1,0:T(8,128)} custom-call(bf16[256,640]{1,0:T(8,128)(2,1)} %q_ref.1, bf16[256,640]{1,0:T(8,128)(2,1)} %k_ref.1, bf16[256,640]{1,0:T(8,128)(2,1)} %v_ref.1, s32[2,16]{1,0:T(2,128)} %lists_ref.1, s32[2]{0:T(128)} %counts_ref.1, bf16[640,1280]{1,0:T(8,128)(2,1)} %w_ref.1), custom_call_target="tpu_custom_call" | custom-call | flops 3825205248 | bytes 2621440 | tf_op jit(solution)/shard_map/pallas_call | solution.py:483
  77.3 0.0 copy-done
  77.3 2.2 %multiply_convert_fusion = bf16[256,1280]{1,0:T(8,128)(2,1)} fusion(f32[256,1280]{1,0:T(8,128)} %shard_map.73, f32[1280]{0:T(1024)S(1)} %copy-done), kind=kLoop, calls=%fused_computation | loop fusion | flops 655360 | bytes 1971200 | tf_op jit(solution)/shard_map/convert_element_type | solution.py:516
Async XLA Ops:
  0.0 77.3 %copy-start = (f32[1280]{0:T(1024)S(1)}, f32[1280]{0:T(1024)}, u32[]{:S(2)}) copy-start(f32[1280]{0:T(1024)} %param.13) | copy-start | bytes 15364

commit v3 on v2

--- a/solution.py
+++ b/solution.py
@@ -120,10 +120,17 @@
                 x_copy(kind, slot, z, d, sources[kind].at[:, cols(my_head(slot))]).start()
         own_copy(kind, slot, my_head(slot)).start()
 
+    def wave(kind, d, act):
+        dst = (z + d) % reps
+        each_base(lambda slot: act(z_copy(kind, slot, slot * reps + dst, dst, z)))
+        for n in range(extra):
+            pl.when((extra_rep(g, reps) + n) % reps == dst)(
+                lambda: act(z_copy(kind, base, base * reps + n, dst, z))
+            )
+
+    for d in range(1, reps):
+        wave(0, d, lambda copy: copy.start())
     for kind in range(3):
-        for d in range(1, reps):
-            dst = (z + d) % reps
-            each_base(lambda slot: z_copy(kind, slot, slot * reps + dst, dst, z).start())
         each_base(lambda slot: start_own(kind, slot))
 
     mate = g + 1 - 2 * (g % 2)
@@ -188,13 +195,6 @@
         mask_copy((z + d) % reps, z).start()
 
     for kind in range(3):
-        for n in range(extra):
-            dst = (extra_rep(g, reps) + n) % reps
-
-            @pl.when(dst != z)
-            def _():
-                z_copy(kind, base, base * reps + n, dst, z).start()
-
         if_extra(lambda slot: start_own(kind, slot))
 
     for piece in range(pieces):
@@ -217,13 +217,10 @@
 
     lax.fori_loop(0, frames, spread_mask, 0)
 
-    def pass_on(slot):
-        for kind in range(2):
-            for d in range(1, reps):
-                src = (z + d) % reps
-                z_copy(kind, slot, 0, z, src).wait_recv()
-                for e in range(1, frames):
-                    x_copy(kind, slot, src, e).start()
+    def pass_on(kind, src, slot):
+        z_copy(kind, slot, 0, z, src).wait_recv()
+        for e in range(1, frames):
+            x_copy(kind, slot, src, e).start()
 
     def rest(slot):
         for kind in range(3):
@@ -293,7 +290,7 @@
             device_id={"heads": other}, device_id_type=MESH,
         ).wait_recv()
 
-    def attend_all(slot):
+    def attend_all(slot, beside=lambda: None):
         def one_chunk(i, _):
             chunk = (z + i) % reps
 
@@ -302,6 +299,7 @@
                 z_copy(2, slot, 0, z, chunk).wait_recv()
 
             attend(slot, chunk)
+            pl.when(i == 0)(beside)
 
             @pl.when(chunk != g)
             def _():
@@ -354,10 +352,15 @@
             def _():
                 line_copy(part, src, -1).start()
 
-    each_base(pass_on)
+    for kind in range(2):
+        for d in range(1, reps):
+            wave(kind, d, lambda copy: copy.wait_send())
+            wave(kind + 1, d, lambda copy: copy.start())
+        for d in range(1, reps):
+            src = (z - d + reps) % reps
+            each_base(lambda slot: pass_on(kind, src, slot))
+            if_extra(lambda slot: pass_on(kind, src, slot))
     each_base(rest)
-    each_base(attend_all)
-    if_extra(pass_on)
 
     def send_on(k, piece):
         w_far(k, piece).wait_recv()
@@ -365,7 +368,7 @@
             w_frame(k, piece, d).start()
         w_mate(k, piece).start()
 
-    w_share(send_on)
+    each_base(lambda slot: attend_all(slot, lambda: w_share(send_on) if slot == 0 else None))
     each_base(lambda slot: att_local(slot).wait())
     for d in range(1, groups):
         each_base(lambda slot: arrive(slot, (g + d) % groups))
@@ -413,17 +416,8 @@
             out_ref[...] += product((z + d) % reps)
 
     for d in range(1, reps):
-        dst = (z + d) % reps
-        mask_copy(dst, z).wait_send()
-        for kind in range(3):
-            each_base(lambda slot: z_copy(kind, slot, slot * reps + dst, dst, z).wait_send())
-    for n in range(extra):
-        dst = (extra_rep(g, reps) + n) % reps
-
-        @pl.when(dst != z)
-        def _():
-            for kind in range(3):
-                z_copy(kind, base, base * reps + n, dst, z).wait_send()
+        mask_copy((z + d) % reps, z).wait_send()
+        wave(2, d, lambda copy: copy.wait_send())
 
     def sent(slot):
         for kind in range(2):

time: 79.7 us -> 76.8 us (0.964)
  the two profiles are of different devices: /device:TPU:7 before, /device:TPU:0 now
where the time goes in v3:
time: 76.8 us; the launch traced here: 75.4 us
  Pallas kernels  73.2 us (95%)
  other arithmetic  2.23 us (3%)
    pallas_call x1, Pallas kernels, shards(): pl.pallas_call(functools.partial(kernel, dims), out_shape=jax.ShapeDtypeS...  73.2 us
    convert_element_type x1, other arithmetic, shards(): return (gate[None, :] * summed).astype(jnp.bfloat16)  2.23 us

profile of v3, /device:TPU:0, one launch (start us, length us, event | category | flops | bytes accessed | tf_op | source)
XLA Modules:
  0.0 75.4 jit_solution(209216519333622125)
XLA Ops:
  0.0 0.0 copy-start
  0.0 73.2 %shard_map.73 = f32[256,1280]{1,0:T(8,128)} custom-call(bf16[256,640]{1,0:T(8,128)(2,1)} %q_ref.1, bf16[256,640]{1,0:T(8,128)(2,1)} %k_ref.1, bf16[256,640]{1,0:T(8,128)(2,1)} %v_ref.1, s32[2,16]{1,0:T(2,128)} %lists_ref.1, s32[2]{0:T(128)} %counts_ref.1, bf16[640,1280]{1,0:T(8,128)(2,1)} %w_ref.1), custom_call_target="tpu_custom_call" | custom-call | flops 3825205248 | bytes 2621440 | tf_op jit(solution)/shard_map/pallas_call | solution.py:477
  73.2 0.0 copy-done
  73.2 2.2 %multiply_convert_fusion = bf16[256,1280]{1,0:T(8,128)(2,1)} fusion(f32[256,1280]{1,0:T(8,128)} %shard_map.73, f32[1280]{0:T(1024)S(1)} %copy-done), kind=kLoop, calls=%fused_computation | loop fusion | flops 655360 | bytes 1971200 | tf_op jit(solution)/shard_map/convert_element_type | solution.py:510
Async XLA Ops:
  0.0 73.2 %copy-start = (f32[1280]{0:T(1024)S(1)}, f32[1280]{0:T(1024)}, u32[]{:S(2)}) copy-start(f32[1280]{0:T(1024)} %param.13) | copy-start | bytes 15364

commit v4 on v3

--- a/solution.py
+++ b/solution.py
@@ -23,7 +23,7 @@
     dims,
     q_ref, k_ref, v_ref, lists_ref, counts_ref, w_ref,
     out_ref,
-    qbuf, kbuf, vbuf, mbuf, bias_buf, stage, abuf, wbuf,
+    qbuf, kbuf, vbuf, vturned, mbuf, stage, abuf, wbuf,
     zs, zr, zms, zmr, xs, xr, own_sem, w_own, ats, atr, gs, gr, wys, wyr, wxs, wxr, wms, wmr,
 ):
     frames, groups, reps, toks, heads, base, extra, parts = dims
@@ -33,7 +33,6 @@
     span = reps * toks
     local_blocks = toks // BLOCK
     frame_blocks = span // BLOCK
-    lanes = mbuf.shape[-1]
     part_cols = w_ref.shape[1] // parts
     halves = groups // 2
 
@@ -182,15 +181,16 @@
 
     w_share(lambda k, piece: w_far(k, piece).start())
 
-    row_id = lax.broadcasted_iota(jnp.int32, (8, lanes), 0)
-    lane_id = lax.broadcasted_iota(jnp.int32, (8, lanes), 1)
-    allowed = jnp.zeros((8, lanes), jnp.float32)
+    blocks = frames * frame_blocks
+    key_block = lax.broadcasted_iota(jnp.int32, (blocks, toks), 0)
+    query_block = lax.broadcasted_iota(jnp.int32, (blocks, toks), 1) // BLOCK
+    term = jnp.full((blocks, toks), -NEG, jnp.float32)
     for b in range(local_blocks):
         used = counts_ref[b]
         for j in range(LIST):
-            hit = (lane_id == lists_ref[b, j]) & (row_id == b) & (jnp.full((8, lanes), j) < used)
-            allowed = jnp.where(hit, 1.0, allowed)
-    mbuf[z] = allowed
+            listed = jnp.where(j < used, lists_ref[b, j], -1)
+            term = jnp.where((key_block == listed) & (query_block == b), 0.0, term)
+    mbuf[z] = term
     for d in range(1, reps):
         mask_copy((z + d) % reps, z).start()
 
@@ -203,19 +203,6 @@
 
     for d in range(1, reps):
         mask_copy(z, (z + d) % reps).wait_recv()
-    mask_rows = mbuf[...].reshape(reps * 8, lanes).astype(jnp.bfloat16)
-    block_of = lax.broadcasted_iota(jnp.int32, (lanes, span), 1) // BLOCK
-    lane_of = lax.broadcasted_iota(jnp.int32, (lanes, span), 0)
-
-    def spread_mask(frame, _):
-        spread = jnp.where(block_of + frame * frame_blocks == lane_of, 1.0, 0.0)
-        hits = jnp.dot(
-            mask_rows, spread.astype(jnp.bfloat16), preferred_element_type=jnp.float32
-        )
-        bias_buf[frame] = (NEG * (hits - 1.0)).reshape(reps, 8, span)
-        return 0
-
-    lax.fori_loop(0, frames, spread_mask, 0)
 
     def pass_on(kind, src, slot):
         z_copy(kind, slot, 0, z, src).wait_recv()
@@ -236,36 +223,56 @@
                         device_id={"tm": (tm + d) % frames}, device_id_type=MESH,
                     ).wait_recv()
 
+    tile = min(span, 256)
+
+    def turn_values(slot):
+        def turn(frame, _):
+            for at in range(0, span, tile):
+                part = vbuf[slot, frame, at : at + tile].astype(jnp.float32)
+                vturned[slot, frame, :, at : at + tile] = part.T.astype(jnp.bfloat16)
+            return 0
+
+        lax.fori_loop(0, frames, turn, 0)
+
     def attend(slot, chunk):
         queries = qbuf[slot, rows(chunk)]
         factor = 1.4426950408889634 / HD**0.5
 
         def step(frame, state):
             top, total, sums = state
-            bias = bias_buf[frame, chunk]
-            scores = lax.dot_general(
-                queries, kbuf[slot, frame], (((1,), (1,)), ((), ())),
-                preferred_element_type=jnp.float32,
-            )
-            scores = scores + jnp.concatenate(
-                [jnp.broadcast_to(bias[b : b + 1], (BLOCK, span)) for b in range(local_blocks)], 0
-            )
-            new_top = jnp.maximum(top, jnp.max(scores, axis=1, keepdims=True))
-            weights = jnp.exp2((scores - new_top) * factor)
+            terms = mbuf[chunk, pl.ds(pl.multiple_of(frame * frame_blocks, frame_blocks), frame_blocks)]
+            tiles = []
+            new_top = top
+            for at in range(0, span, tile):
+                scores = lax.dot_general(
+                    kbuf[slot, frame, at : at + tile], queries, (((1,), (1,)), ((), ())),
+                    preferred_element_type=jnp.float32,
+                )
+                own_terms = terms[at // BLOCK : (at + tile) // BLOCK]
+                scores = scores.reshape(tile // BLOCK, BLOCK, toks) + own_terms[:, None, :]
+                scores = scores.reshape(tile, toks)
+                new_top = jnp.maximum(new_top, jnp.max(scores, axis=0, keepdims=True))
+                tiles.append(scores)
             scale = jnp.exp2((top - new_top) * factor)
-            total = total * scale + jnp.sum(weights, axis=1, keepdims=True)
-            sums = sums * scale + jnp.dot(
-                weights.astype(jnp.bfloat16), vbuf[slot, frame], preferred_element_type=jnp.float32
-            )
+            total = total * scale
+            sums = sums * scale
+            for n, scores in enumerate(tiles):
+                weights = jnp.exp2((scores - new_top) * factor)
+                total = total + jnp.sum(weights, axis=0, keepdims=True)
+                sums = sums + jnp.dot(
+                    vturned[slot, frame, :, n * tile : (n + 1) * tile],
+                    weights.astype(jnp.bfloat16),
+                    preferred_element_type=jnp.float32,
+                )
             return new_top, total, sums
 
         state = (
-            jnp.full((toks, 1), -NEG, jnp.float32),
-            jnp.zeros((toks, 1), jnp.float32),
-            jnp.zeros((toks, HD), jnp.float32),
+            jnp.full((1, toks), -NEG, jnp.float32),
+            jnp.zeros((1, toks), jnp.float32),
+            jnp.zeros((HD, toks), jnp.float32),
         )
         _, total, sums = lax.fori_loop(0, frames, step, state, unroll=min(frames, 2))
-        stage[slot, rows(chunk)] = (sums / total).astype(jnp.bfloat16)
+        stage[slot, rows(chunk)] = (sums / total).T.astype(jnp.bfloat16)
 
     def position(slot, group):
         return slot * groups + group if slot < base else base * groups + extra_rank(z, group)
@@ -311,6 +318,7 @@
 
             return 0
 
+        turn_values(slot)
         lax.fori_loop(0, reps, one_chunk, 0)
 
     line_cols = (pl.ds(0, base * groups * HD), pl.ds(base * groups * HD, (heads - base * reps) * HD))
@@ -462,7 +470,6 @@
     assert groups == reps and groups % 2 == 0
     plane_heads = heads * groups // reps
     span = reps * toks
-    lanes = -(-(span * frames // BLOCK) // 128) * 128
     parts = 2 if wide % 256 == 0 else 1
     dims = (frames, groups, reps, toks, heads, base, extra, parts)
     others = max(frames - 1, 1)
@@ -483,8 +490,8 @@
             pltpu.VMEM((slots, span, HD), jnp.bfloat16),
             pltpu.VMEM((slots, frames, span, HD), jnp.bfloat16),
             pltpu.VMEM((slots, frames, span, HD), jnp.bfloat16),
-            pltpu.VMEM((reps, 8, lanes), jnp.float32),
-            pltpu.VMEM((frames, reps, 8, span), jnp.float32),
+            pltpu.VMEM((slots, frames, HD, span), jnp.bfloat16),
+            pltpu.VMEM((reps, span * frames // BLOCK, toks), jnp.float32),
             pltpu.VMEM((slots, span, HD), jnp.bfloat16),
             pltpu.VMEM((reps, toks, plane_heads * HD), jnp.bfloat16),
             pltpu.VMEM((reps, plane_heads * HD, wide), jnp.bfloat16),

time: 76.8 us -> 77.5 us (level); the launches traced: 75.4 us -> 77.4 us
  Pallas kernels: 73.2 us -> 75.1 us
    pallas_call x1, Pallas kernels: 73.2 us -> 75.1 us  [shards(): pl.pallas_call(functools.partial(kernel, dims), out_shape=jax.ShapeDtypeS...]
where the time goes in v4:
time: 77.5 us; the launch traced here: 77.4 us
  Pallas kernels  75.1 us (97%)
  other arithmetic  2.23 us (3%)
    pallas_call x1, Pallas kernels, shards(): pl.pallas_call(functools.partial(kernel, dims), out_shape=jax.ShapeDtypeS...  75.1 us
    convert_element_type x1, other arithmetic, shards(): return (gate[None, :] * summed).astype(jnp.bfloat16)  2.23 us

profile of v4, /device:TPU:0, one launch (start us, length us, event | category | flops | bytes accessed | tf_op | source)
XLA Modules:
  0.0 77.4 jit_solution(12388973794154500336)
XLA Ops:
  0.0 0.0 copy-start
  0.0 75.1 %shard_map.73 = f32[256,1280]{1,0:T(8,128)} custom-call(bf16[256,640]{1,0:T(8,128)(2,1)} %q_ref.1, bf16[256,640]{1,0:T(8,128)(2,1)} %k_ref.1, bf16[256,640]{1,0:T(8,128)(2,1)} %v_ref.1, s32[2,16]{1,0:T(2,128)} %lists_ref.1, s32[2]{0:T(128)} %counts_ref.1, bf16[640,1280]{1,0:T(8,128)(2,1)} %w_ref.1), custom_call_target="tpu_custom_call" | custom-call | flops 3825205248 | bytes 2621440 | tf_op jit(solution)/shard_map/pallas_call | solution.py:484
  75.1 0.0 copy-done
  75.1 2.2 %multiply_convert_fusion = bf16[256,1280]{1,0:T(8,128)(2,1)} fusion(f32[256,1280]{1,0:T(8,128)} %shard_map.73, f32[1280]{0:T(1024)S(1)} %copy-done), kind=kLoop, calls=%fused_computation | loop fusion | flops 655360 | bytes 1971200 | tf_op jit(solution)/shard_map/convert_element_type | solution.py:517
Async XLA Ops:
  0.0 75.1 %copy-start = (f32[1280]{0:T(1024)S(1)}, f32[1280]{0:T(1024)}, u32[]{:S(2)}) copy-start(f32[1280]{0:T(1024)} %param.13) | copy-start | bytes 15364

commit v5 on v4

--- a/solution.py
+++ b/solution.py
@@ -33,7 +33,7 @@
     span = reps * toks
     local_blocks = toks // BLOCK
     frame_blocks = span // BLOCK
-    part_cols = w_ref.shape[1] // parts
+    part_rows = w_ref.shape[0] // parts
     halves = groups // 2
 
     def cols(head):
@@ -54,11 +54,17 @@
     my_extra = extra_of(g)
     has_extra = my_extra < extra
 
-    def place(group, head):
-        if head < base * reps:
-            return head % reps, (head // reps) * groups + group
-        plane = (extra_rep(group, reps) + head - base * reps) % reps
-        return plane, base * groups + extra_rank(plane, group)
+    def extra_owner(plane, position):
+        owner = sum(
+            jnp.where(
+                ((plane - extra_rep(other, reps) + reps) % reps < extra)
+                & (extra_rank(plane, other) == position),
+                other,
+                0,
+            )
+            for other in range(groups)
+        )
+        return owner, base * reps + (plane - extra_rep(owner, reps) + reps) % reps
 
     barrier = pltpu.get_barrier_semaphore()
     for axis, count, me in (("rep", reps, z), ("tm", frames, tm), ("heads", groups, g)):
@@ -66,121 +72,6 @@
             pl.semaphore_signal(
                 barrier, inc=1, device_id={axis: (me + d) % count}, device_id_type=MESH
             )
-    pl.semaphore_wait(barrier, reps + frames + groups - 3)
-
-    def mask_copy(dst, src):
-        return pltpu.make_async_remote_copy(
-            src_ref=mbuf.at[src], dst_ref=mbuf.at[src],
-            send_sem=zms.at[dst], recv_sem=zmr.at[src],
-            device_id={"rep": dst}, device_id_type=MESH,
-        )
-
-    sources = (k_ref, v_ref, q_ref)
-
-    def landing(kind, slot, rep):
-        if kind == 2:
-            return qbuf.at[slot, rows(rep)]
-        return (kbuf, vbuf)[kind].at[slot, tm, rows(rep)]
-
-    def z_copy(kind, slot, head, dst, src):
-        return pltpu.make_async_remote_copy(
-            src_ref=sources[kind].at[:, cols(head)], dst_ref=landing(kind, slot, src),
-            send_sem=zs.at[kind, slot, dst], recv_sem=zr.at[kind, slot, src],
-            device_id={"rep": dst}, device_id_type=MESH,
-        )
-
-    def own_copy(kind, slot, head):
-        return pltpu.make_async_copy(
-            sources[kind].at[:, cols(head)], landing(kind, slot, z), own_sem.at[kind, slot]
-        )
-
-    def x_copy(kind, slot, rep, d, src=None):
-        there = landing(kind, slot, rep)
-        return pltpu.make_async_remote_copy(
-            src_ref=there if src is None else src, dst_ref=there,
-            send_sem=xs.at[kind, slot, rep, d - 1], recv_sem=xr.at[kind, slot, rep, d - 1],
-            device_id={"tm": (tm + d) % frames}, device_id_type=MESH,
-        )
-
-    def my_head(slot):
-        return slot * reps + z if slot < base else base * reps + my_extra
-
-    def if_extra(act):
-        if extra:
-            pl.when(has_extra)(lambda: act(base))
-
-    def each_base(act):
-        for slot in range(base):
-            act(slot)
-
-    def start_own(kind, slot):
-        if kind < 2:
-            for d in range(1, frames):
-                x_copy(kind, slot, z, d, sources[kind].at[:, cols(my_head(slot))]).start()
-        own_copy(kind, slot, my_head(slot)).start()
-
-    def wave(kind, d, act):
-        dst = (z + d) % reps
-        each_base(lambda slot: act(z_copy(kind, slot, slot * reps + dst, dst, z)))
-        for n in range(extra):
-            pl.when((extra_rep(g, reps) + n) % reps == dst)(
-                lambda: act(z_copy(kind, base, base * reps + n, dst, z))
-            )
-
-    for d in range(1, reps):
-        wave(0, d, lambda copy: copy.start())
-    for kind in range(3):
-        each_base(lambda slot: start_own(kind, slot))
-
-    mate = g + 1 - 2 * (g % 2)
-    pieces = heads * parts
-
-    def w_here(piece):
-        return w_ref.at[
-            pl.ds(piece // parts * HD, HD), pl.ds(piece % parts * part_cols, part_cols)
-        ]
-
-    def w_there(group, piece):
-        plane, at = place(group, piece // parts)
-        return wbuf.at[plane, cols(at), pl.ds(piece % parts * part_cols, part_cols)]
-
-    def w_far(k, piece):
-        return pltpu.make_async_remote_copy(
-            src_ref=w_here(piece), dst_ref=w_there(g, piece),
-            send_sem=wys.at[k - 1, piece], recv_sem=wyr.at[k - 1, piece],
-            device_id={"heads": (g + 2 * k) % groups}, device_id_type=MESH,
-        )
-
-    def w_frame(k, piece, d):
-        there = w_there((g - 2 * k + groups) % groups, piece)
-        return pltpu.make_async_remote_copy(
-            src_ref=there, dst_ref=there,
-            send_sem=wxs.at[k - 1, piece, d - 1], recv_sem=wxr.at[k - 1, piece],
-            device_id={"tm": (tm + d) % frames}, device_id_type=MESH,
-        )
-
-    def w_mate(k, piece):
-        there = w_there((g - 2 * k + groups) % groups, piece)
-        return pltpu.make_async_remote_copy(
-            src_ref=there if k else w_here(piece), dst_ref=there,
-            send_sem=wms.at[k, piece], recv_sem=wmr.at[k, piece],
-            device_id={"heads": mate}, device_id_type=MESH,
-        )
-
-    def w_local(piece):
-        return pltpu.make_async_copy(w_here(piece), w_there(g, piece), w_own.at[piece])
-
-    def w_share(act, mine=True):
-        for piece in range(pieces):
-            fetch = tm == piece % frames
-
-            @pl.when(fetch if mine else jnp.logical_not(fetch))
-            def _():
-                for k in range(1, halves):
-                    act(k, piece)
-
-    w_share(lambda k, piece: w_far(k, piece).start())
-
     blocks = frames * frame_blocks
     key_block = lax.broadcasted_iota(jnp.int32, (blocks, toks), 0)
     query_block = lax.broadcasted_iota(jnp.int32, (blocks, toks), 1) // BLOCK
@@ -191,18 +82,123 @@
             listed = jnp.where(j < used, lists_ref[b, j], -1)
             term = jnp.where((key_block == listed) & (query_block == b), 0.0, term)
     mbuf[z] = term
+    pl.semaphore_wait(barrier, reps + frames + groups - 3)
+
+    def mask_copy(dst, src):
+        return pltpu.make_async_remote_copy(
+            src_ref=mbuf.at[src], dst_ref=mbuf.at[src],
+            send_sem=zms.at[dst], recv_sem=zmr.at[src],
+            device_id={"rep": dst}, device_id_type=MESH,
+        )
+
+    sources = (k_ref, v_ref, q_ref)
+
+    def landing(kind, slot, rep):
+        if kind == 2:
+            return qbuf.at[slot, rows(rep)]
+        return (kbuf, vbuf)[kind].at[slot, tm, rows(rep)]
+
+    def z_copy(kind, slot, head, dst, src):
+        return pltpu.make_async_remote_copy(
+            src_ref=sources[kind].at[:, cols(head)], dst_ref=landing(kind, slot, src),
+            send_sem=zs.at[kind, slot, dst], recv_sem=zr.at[kind, slot, src],
+            device_id={"rep": dst}, device_id_type=MESH,
+        )
+
+    def own_copy(kind, slot, head):
+        return pltpu.make_async_copy(
+            sources[kind].at[:, cols(head)], landing(kind, slot, z), own_sem.at[kind, slot]
+        )
+
+    def x_copy(kind, slot, rep, d, src=None):
+        there = landing(kind, slot, rep)
+        return pltpu.make_async_remote_copy(
+            src_ref=there if src is None else src, dst_ref=there,
+            send_sem=xs.at[kind, slot, rep, d - 1], recv_sem=xr.at[kind, slot, rep, d - 1],
+            device_id={"tm": (tm + d) % frames}, device_id_type=MESH,
+        )
+
+    def my_head(slot):
+        return slot * reps + z if slot < base else base * reps + my_extra
+
+    def if_extra(act):
+        if extra:
+            pl.when(has_extra)(lambda: act(base))
+
+    def each_base(act):
+        for slot in range(base):
+            act(slot)
+
+    def start_own(kind, slot):
+        if kind < 2:
+            for d in range(1, frames):
+                x_copy(kind, slot, z, d, sources[kind].at[:, cols(my_head(slot))]).start()
+        own_copy(kind, slot, my_head(slot)).start()
+
+    def wave(kind, d, act):
+        dst = (z + d) % reps
+        each_base(lambda slot: act(z_copy(kind, slot, slot * reps + dst, dst, z)))
+        for n in range(extra):
+            pl.when((extra_rep(g, reps) + n) % reps == dst)(
+                lambda: act(z_copy(kind, base, base * reps + n, dst, z))
+            )
+
+    for d in range(1, reps):
+        wave(0, d, lambda copy: copy.start())
+    for kind in range(3):
+        each_base(lambda slot: start_own(kind, slot))
+
+    mate = g + 1 - 2 * (g % 2)
+    pieces = parts
+
+    def w_here(piece):
+        return w_ref.at[pl.ds(piece * part_rows, part_rows)]
+
+    def w_there(group, piece):
+        return wbuf.at[group, pl.ds(piece * part_rows, part_rows)]
+
+    def w_far(k, piece):
+        return pltpu.make_async_remote_copy(
+            src_ref=w_here(piece), dst_ref=w_there(g, piece),
+            send_sem=wys.at[k - 1, piece], recv_sem=wyr.at[k - 1, piece],
+            device_id={"heads": (g + 2 * k) % groups}, device_id_type=MESH,
+        )
+
+    def w_frame(k, piece, d):
+        there = w_there((g - 2 * k + groups) % groups, piece)
+        return pltpu.make_async_remote_copy(
+            src_ref=there, dst_ref=there,
+            send_sem=wxs.at[k - 1, piece, d - 1], recv_sem=wxr.at[k - 1, piece],
+            device_id={"tm": (tm + d) % frames}, device_id_type=MESH,
+        )
+
+    def w_mate(k, piece):
+        there = w_there((g - 2 * k + groups) % groups, piece)
+        return pltpu.make_async_remote_copy(
+            src_ref=there if k else w_here(piece), dst_ref=there,
+            send_sem=wms.at[k, piece], recv_sem=wmr.at[k, piece],
+            device_id={"heads": mate}, device_id_type=MESH,
+        )
+
+    def w_local(piece):
+        return pltpu.make_async_copy(w_here(piece), w_there(g, piece), w_own.at[piece])
+
+    def w_share(act, mine=True):
+        for piece in range(pieces):
+            fetch = tm == piece % frames
+
+            @pl.when(fetch if mine else jnp.logical_not(fetch))
+            def _():
+                for k in range(1, halves):
+                    act(k, piece)
+
+    w_share(lambda k, piece: w_far(k, piece).start())
+
     for d in range(1, reps):
         mask_copy((z + d) % reps, z).start()
 
     for kind in range(3):
         if_extra(lambda slot: start_own(kind, slot))
-
-    for piece in range(pieces):
-        w_mate(0, piece).start()
-        w_local(piece).start()
-
-    for d in range(1, reps):
-        mask_copy(z, (z + d) % reps).wait_recv()
 
     def pass_on(kind, src, slot):
         z_copy(kind, slot, 0, z, src).wait_recv()
@@ -368,6 +364,13 @@
             src = (z - d + reps) % reps
             each_base(lambda slot: pass_on(kind, src, slot))
             if_extra(lambda slot: pass_on(kind, src, slot))
+    for piece in range(pieces):
+        w_mate(0, piece).start()
+        w_local(piece).start()
+
+    for d in range(1, reps):
+        mask_copy(z, (z + d) % reps).wait_recv()
+
     each_base(rest)
 
     def send_on(k, piece):
@@ -381,6 +384,10 @@
     for d in range(1, groups):
         each_base(lambda slot: arrive(slot, (g + d) % groups))
     line_start(0)
+
+    def to_mate(k, piece):
+        w_frame(k, piece, 1).wait_recv()
+        w_mate(k, piece).start()
 
     if_extra(rest)
     if_extra(attend_all)
@@ -392,22 +399,30 @@
                 other = (g + e) % groups
                 pl.when(extra_of(other) < extra)(lambda: arrive(base, other))
             line_start(1)
+        if d == 1:
+            w_share(to_mate, mine=False)
     if extra:
         for d in range(1, reps - 1):
             line_relay(1, d)
 
-    def to_mate(k, piece):
-        w_frame(k, piece, 1).wait_recv()
-        w_mate(k, piece).start()
-
-    w_share(to_mate, mine=False)
     for piece in range(pieces):
         for k in range(halves):
             w_mate(k, piece).wait_recv()
         w_local(piece).wait()
 
     def product(src):
-        return jnp.dot(abuf[src], wbuf[src], preferred_element_type=jnp.float32)
+        total = None
+        for at in range(abuf.shape[2] // HD):
+            if at < base * groups:
+                group, head = at % groups, (at // groups) * reps + src
+            else:
+                group, head = extra_owner(src, at - base * groups)
+            term = jnp.dot(
+                abuf[src, :, at * HD : (at + 1) * HD], wbuf[group, cols(head)],
+                preferred_element_type=jnp.float32,
+            )
+            total = term if total is None else total + term
+        return total
 
     out_ref[...] = product(z)
     for d in range(1, reps):
@@ -470,12 +485,12 @@
     assert groups == reps and groups % 2 == 0
     plane_heads = heads * groups // reps
     span = reps * toks
-    parts = 2 if wide % 256 == 0 else 1
+    parts = 2 if out_weight.shape[0] % 32 == 0 else 1
     dims = (frames, groups, reps, toks, heads, base, extra, parts)
     others = max(frames - 1, 1)
     halves = groups // 2
     far = max(halves - 1, 1)
-    pieces = heads * parts
+    pieces = parts
     vmem, smem, hbm = (
         pl.BlockSpec(memory_space=m) for m in (pltpu.VMEM, pltpu.SMEM, pl.ANY)
     )
@@ -494,7 +509,7 @@
             pltpu.VMEM((reps, span * frames // BLOCK, toks), jnp.float32),
             pltpu.VMEM((slots, span, HD), jnp.bfloat16),
             pltpu.VMEM((reps, toks, plane_heads * HD), jnp.bfloat16),
-            pltpu.VMEM((reps, plane_heads * HD, wide), jnp.bfloat16),
+            pltpu.VMEM((groups, heads * HD, wide), jnp.bfloat16),
             dma((3, slots, reps)), dma((3, slots, reps)),
             dma((reps,)), dma((reps,)),
             dma((2, slots, reps, others)), dma((2, slots, reps, others)),

time: 77.5 us -> 72.9 us (0.941)
  Pallas kernels: 75.1 us -> 70.4 us
    pallas_call x1, Pallas kernels: 75.1 us -> 70.4 us  [shards(): pl.pallas_call(functools.partial(kernel, dims), out_shape=jax.ShapeDtypeS...]
where the time goes in v5:
time: 72.9 us; the launch traced here: 72.7 us
  Pallas kernels  70.4 us (97%)
  other arithmetic  2.23 us (3%)
    pallas_call x1, Pallas kernels, shards(): pl.pallas_call(functools.partial(kernel, dims), out_shape=jax.ShapeDtypeS...  70.4 us
    convert_element_type x1, other arithmetic, shards(): return (gate[None, :] * summed).astype(jnp.bfloat16)  2.23 us

profile of v5, /device:TPU:0, one launch (start us, length us, event | category | flops | bytes accessed | tf_op | source)
XLA Modules:
  0.0 72.7 jit_solution(11858161708405073221)
XLA Ops:
  0.0 0.0 copy-start
  0.0 70.4 %shard_map.73 = f32[256,1280]{1,0:T(8,128)} custom-call(bf16[256,640]{1,0:T(8,128)(2,1)} %q_ref.1, bf16[256,640]{1,0:T(8,128)(2,1)} %k_ref.1, bf16[256,640]{1,0:T(8,128)(2,1)} %v_ref.1, s32[2,16]{1,0:T(2,128)} %lists_ref.1, s32[2]{0:T(128)} %counts_ref.1, bf16[640,1280]{1,0:T(8,128)(2,1)} %w_ref.1), custom_call_target="tpu_custom_call" | custom-call | flops 3825205248 | bytes 2621440 | tf_op jit(solution)/shard_map/pallas_call | solution.py:499
  70.4 0.0 copy-done
  70.4 2.2 %multiply_convert_fusion = bf16[256,1280]{1,0:T(8,128)(2,1)} fusion(f32[256,1280]{1,0:T(8,128)} %shard_map.73, f32[1280]{0:T(1024)S(1)} %copy-done), kind=kLoop, calls=%fused_computation | loop fusion | flops 655360 | bytes 1971200 | tf_op jit(solution)/shard_map/convert_element_type | solution.py:532
Async XLA Ops:
  0.0 70.4 %copy-start = (f32[1280]{0:T(1024)S(1)}, f32[1280]{0:T(1024)}, u32[]{:S(2)}) copy-start(f32[1280]{0:T(1024)} %param.13) | copy-start | bytes 15364

commit v6 on v5

--- a/solution.py
+++ b/solution.py
@@ -393,18 +393,15 @@
     if_extra(attend_all)
     for d in range(1, reps - 1):
         line_relay(0, d)
-        if d == 1 and extra:
-            if_extra(lambda slot: att_local(slot).wait())
-            for e in range(1, groups):
-                other = (g + e) % groups
-                pl.when(extra_of(other) < extra)(lambda: arrive(base, other))
-            line_start(1)
-        if d == 1:
-            w_share(to_mate, mine=False)
     if extra:
+        if_extra(lambda slot: att_local(slot).wait())
+        for e in range(1, groups):
+            other = (g + e) % groups
+            pl.when(extra_of(other) < extra)(lambda: arrive(base, other))
+        line_start(1)
         for d in range(1, reps - 1):
             line_relay(1, d)
-
+    w_share(to_mate, mine=False)
     for piece in range(pieces):
         for k in range(halves):
             w_mate(k, piece).wait_recv()

time: 72.9 us -> 74.9 us (1.027)
  the two profiles are of different devices: /device:TPU:0 before, /device:TPU:29 now
where the time goes in v6:
time: 74.9 us; the launch traced here: 74.7 us
  Pallas kernels  72.4 us (97%)
  other arithmetic  2.23 us (3%)
    pallas_call x1, Pallas kernels, shards(): pl.pallas_call(functools.partial(kernel, dims), out_shape=jax.ShapeDtypeS...  72.4 us
    convert_element_type x1, other arithmetic, shards(): return (gate[None, :] * summed).astype(jnp.bfloat16)  2.23 us

profile of v6, /device:TPU:29, one launch (start us, length us, event | category | flops | bytes accessed | tf_op | source)
XLA Modules:
  0.0 74.7 jit_solution(4041747547538222817)
XLA Ops:
  0.0 0.0 copy-start
  0.0 72.4 %shard_map.73 = f32[256,1280]{1,0:T(8,128)} custom-call(bf16[256,640]{1,0:T(8,128)(2,1)} %q_ref.1, bf16[256,640]{1,0:T(8,128)(2,1)} %k_ref.1, bf16[256,640]{1,0:T(8,128)(2,1)} %v_ref.1, s32[2,16]{1,0:T(2,128)} %lists_ref.1, s32[2]{0:T(128)} %counts_ref.1, bf16[640,1280]{1,0:T(8,128)(2,1)} %w_ref.1), custom_call_target="tpu_custom_call" | custom-call | flops 3825205248 | bytes 2621440 | tf_op jit(solution)/shard_map/pallas_call | solution.py:496
  72.5 0.0 copy-done
  72.5 2.2 %multiply_convert_fusion = bf16[256,1280]{1,0:T(8,128)(2,1)} fusion(f32[256,1280]{1,0:T(8,128)} %shard_map.73, f32[1280]{0:T(1024)S(1)} %copy-done), kind=kLoop, calls=%fused_computation | loop fusion | flops 655360 | bytes 1971200 | tf_op jit(solution)/shard_map/convert_element_type | solution.py:529
Async XLA Ops:
  0.0 72.5 %copy-start = (f32[1280]{0:T(1024)S(1)}, f32[1280]{0:T(1024)}, u32[]{:S(2)}) copy-start(f32[1280]{0:T(1024)} %param.13) | copy-start | bytes 15364

commit v7 on v6

--- a/solution.py
+++ b/solution.py
@@ -391,16 +391,15 @@
 
     if_extra(rest)
     if_extra(attend_all)
-    for d in range(1, reps - 1):
-        line_relay(0, d)
     if extra:
         if_extra(lambda slot: att_local(slot).wait())
         for e in range(1, groups):
             other = (g + e) % groups
             pl.when(extra_of(other) < extra)(lambda: arrive(base, other))
         line_start(1)
-        for d in range(1, reps - 1):
-            line_relay(1, d)
+    for d in range(1, reps - 1):
+        for part in range(line_parts):
+            line_relay(part, d)
     w_share(to_mate, mine=False)
     for piece in range(pieces):
         for k in range(halves):

time: 74.9 us -> 69.9 us (0.933)
  the two profiles are of different devices: /device:TPU:29 before, /device:TPU:0 now
where the time goes in v7:
time: 69.9 us; the launch traced here: 69.7 us
  Pallas kernels  67.5 us (97%)
  other arithmetic  2.23 us (3%)
    pallas_call x1, Pallas kernels, shards(): pl.pallas_call(functools.partial(kernel, dims), out_shape=jax.ShapeDtypeS...  67.5 us
    convert_element_type x1, other arithmetic, shards(): return (gate[None, :] * summed).astype(jnp.bfloat16)  2.23 us

profile of v7, /device:TPU:0, one launch (start us, length us, event | category | flops | bytes accessed | tf_op | source)
XLA Modules:
  0.0 69.7 jit_solution(12379978039268975973)
XLA Ops:
  0.0 0.0 copy-start
  0.0 67.5 %shard_map.73 = f32[256,1280]{1,0:T(8,128)} custom-call(bf16[256,640]{1,0:T(8,128)(2,1)} %q_ref.1, bf16[256,640]{1,0:T(8,128)(2,1)} %k_ref.1, bf16[256,640]{1,0:T(8,128)(2,1)} %v_ref.1, s32[2,16]{1,0:T(2,128)} %lists_ref.1, s32[2]{0:T(128)} %counts_ref.1, bf16[640,1280]{1,0:T(8,128)(2,1)} %w_ref.1), custom_call_target="tpu_custom_call" | custom-call | flops 3825205248 | bytes 2621440 | tf_op jit(solution)/shard_map/pallas_call | solution.py:495
  67.5 0.0 copy-done
  67.5 2.2 %multiply_convert_fusion = bf16[256,1280]{1,0:T(8,128)(2,1)} fusion(f32[256,1280]{1,0:T(8,128)} %shard_map.73, f32[1280]{0:T(1024)S(1)} %copy-done), kind=kLoop, calls=%fused_computation | loop fusion | flops 655360 | bytes 1971200 | tf_op jit(solution)/shard_map/convert_element_type | solution.py:528
Async XLA Ops:
  0.0 67.5 %copy-start = (f32[1280]{0:T(1024)S(1)}, f32[1280]{0:T(1024)}, u32[]{:S(2)}) copy-start(f32[1280]{0:T(1024)} %param.13) | copy-start | bytes 15364

commit v8 on v7

--- a/solution.py
+++ b/solution.py
@@ -302,7 +302,6 @@
                 z_copy(2, slot, 0, z, chunk).wait_recv()
 
             attend(slot, chunk)
-            pl.when(i == 0)(beside)
 
             @pl.when(chunk != g)
             def _():
@@ -312,6 +311,7 @@
             def _():
                 att_local(slot).start()
 
+            pl.when(i == max(reps - 2, 0))(beside)
             return 0
 
         turn_values(slot)

time: 69.9 us -> 70 us (level)
  no operation moved by 1% of the time
where the time goes in v8:
time: 70 us; the launch traced here: 69.8 us
  Pallas kernels  67.6 us (97%)
  other arithmetic  2.23 us (3%)
    pallas_call x1, Pallas kernels, shards(): pl.pallas_call(functools.partial(kernel, dims), out_shape=jax.ShapeDtypeS...  67.6 us
    convert_element_type x1, other arithmetic, shards(): return (gate[None, :] * summed).astype(jnp.bfloat16)  2.23 us

profile of v8, /device:TPU:0, one launch (start us, length us, event | category | flops | bytes accessed | tf_op | source)
XLA Modules:
  0.0 69.8 jit_solution(10134409603870047068)
XLA Ops:
  0.0 0.0 copy-start
  0.0 67.6 %shard_map.73 = f32[256,1280]{1,0:T(8,128)} custom-call(bf16[256,640]{1,0:T(8,128)(2,1)} %q_ref.1, bf16[256,640]{1,0:T(8,128)(2,1)} %k_ref.1, bf16[256,640]{1,0:T(8,128)(2,1)} %v_ref.1, s32[2,16]{1,0:T(2,128)} %lists_ref.1, s32[2]{0:T(128)} %counts_ref.1, bf16[640,1280]{1,0:T(8,128)(2,1)} %w_ref.1), custom_call_target="tpu_custom_call" | custom-call | flops 3825205248 | bytes 2621440 | tf_op jit(solution)/shard_map/pallas_call | solution.py:495
  67.6 0.0 copy-done
  67.6 2.2 %multiply_convert_fusion = bf16[256,1280]{1,0:T(8,128)(2,1)} fusion(f32[256,1280]{1,0:T(8,128)} %shard_map.73, f32[1280]{0:T(1024)S(1)} %copy-done), kind=kLoop, calls=%fused_computation | loop fusion | flops 655360 | bytes 1971200 | tf_op jit(solution)/shard_map/convert_element_type | solution.py:528
Async XLA Ops:
  0.0 67.6 %copy-start = (f32[1280]{0:T(1024)S(1)}, f32[1280]{0:T(1024)}, u32[]{:S(2)}) copy-start(f32[1280]{0:T(1024)} %param.13) | copy-start | bytes 15364
